TPU v7x, 32 devices: a whole 2x2x4 slice. The times are simulated.
32 devices in a mesh: blk: 32 (over z, y, x, core), mp: 1.
Axes of the slice: x: 2, y: 2, z: 4, core: 2. Of those that a mesh axis runs over, the one named last changes fastest.
Arguments:
- tokens: bfloat16 [8192, 2048], P('blk'), may hold values from -6 to 6
- attn_gain: float32 [2048], replicated, may hold values from 0.1 to 1.9
- w_qkv: bfloat16 [2048, 3, 2048], P(None, None, 'mp'), may hold values from -4 to 4
- w_o: bfloat16 [2048, 2048], P('mp'), may hold values from -2.5 to 2.5
- moe_gain: float32 [2048], replicated, may hold values from 0.1 to 1.9
- w_gate_up: bfloat16 [64, 2048, 2, 1408], P('blk', None, None, 'mp'), may hold values from -0.125 to 0.125
- w_down: bfloat16 [64, 1408, 2048], P('blk', 'mp'), may hold values from -0.15625 to 0.15625
- expert_ids: int32 [8192, 6], P(('blk', 'mp')), may hold values from 0 to 63, all different within a row; in each aligned block of 256 rows (0 to 255, 256 to 511, ...) at most 40 rows name the same one
- gate_weights: bfloat16 [8192, 6], P(('blk', 'mp')), may hold values from 0.049804688 to 0.5
- prompt_lengths: int32 [4], replicated, may hold values from 1 to 4096, 8192 in all
- page_table: int32 [64], P('blk'), may hold values from 0 to 63, each once
Outputs:
- mixed: bfloat16 [8192, 2048], P(('blk', 'mp'))
- kv_cache: bfloat16 [64, 2, 128, 2048], P('blk', None, None, 'mp')
Inputs may be any that keep to these rules, and one draw needn't show every extreme that they name: `expert_ids`: each row names 6 different experts; within the rows of one device (aligned blocks of 256 rows) no expert is named by more than 40 rows, a bound that some block reaches. `prompt_lengths`: the lengths sum to 8192; the longest is exactly 4096. `page_table`: each page number appears once.
All inputs are finite; a program needn't handle non-finite values.
Results may differ from a plain program's by a relative error of at most 0.017.
Values may be sent and summed in bfloat16 or wider, within the bound.
No kernel may reach another device: no remote copies, remote signals or barrier semaphores. Data moves between devices by JAX's collectives and lax.ppermute only.
A program may use at most 320 MiB of HBM per device.

v0:
```python
import math

import jax
import jax.numpy as jnp
from jax import lax
from jax.sharding import PartitionSpec as P

HD = 128
TOP = 6
PAGE = 128


EPS = 1e-06
THETA = 10000.0
NEG = -1e30


def rms_scale(values, gain):
    mean_sq = jnp.mean(values * values, axis=-1, keepdims=True)
    return values * lax.rsqrt(mean_sq + EPS) * gain


def rotate(values, relative):
    halfd = values.shape[-1] // 2
    inverse = THETA ** (-jnp.arange(halfd, dtype=jnp.float32) / halfd)
    angle = relative.astype(jnp.float32)[:, None] * inverse[None, :]
    cosine = jnp.cos(angle)[:, None, :]
    sine = jnp.sin(angle)[:, None, :]
    first = values[..., :halfd]
    second = values[..., halfd:]
    return jnp.concatenate(
        [first * cosine - second * sine, second * cosine + first * sine], axis=-1
    )


def row_positions(rows, tok_rows, blocks):
    half = tok_rows // 2
    device = rows // tok_rows
    inner = rows % tok_rows
    return jnp.where(
        inner < half, device * half + inner, (2 * blocks - 1 - device) * half + inner - half
    )


def tenant_info(positions, prompt_lengths):
    starts = jnp.cumsum(prompt_lengths) - prompt_lengths
    after = starts[None, :] <= positions[:, None]
    prompt = jnp.sum(after.astype(jnp.int32), axis=1) - 1
    begin = jnp.max(jnp.where(after, starts[None, :], 0), axis=1)
    return (prompt, positions - begin)


def body(
    tokens,
    attn_gain,
    w_qkv,
    w_o,
    moe_gain,
    w_gate_up,
    w_down,
    expert_ids,
    gate_weights,
    prompt_lengths,
    page_table,
):
    blocks = lax.axis_size("blk")
    shares = lax.axis_size("mp")
    block_id = lax.axis_index("blk")
    share_id = lax.axis_index("mp")
    tok_rows, width = tokens.shape
    half = tok_rows // 2
    head_cols = w_qkv.shape[2]
    local_heads = head_cols // HD
    own_rows = block_id * tok_rows + jnp.arange(tok_rows, dtype=jnp.int32)
    own_pos = row_positions(own_rows, tok_rows, blocks)
    own_prompt, relative = tenant_info(own_pos, prompt_lengths)
    normed = rms_scale(tokens.astype(jnp.float32), attn_gain).astype(jnp.bfloat16)
    projected = jnp.dot(
        normed, w_qkv.reshape(width, 3 * head_cols), preferred_element_type=jnp.float32
    ).reshape(tok_rows, 3, local_heads, HD)
    query = rotate(projected[:, 0], relative).astype(jnp.bfloat16)
    keys = rotate(projected[:, 1], relative).astype(jnp.bfloat16).reshape(tok_rows, head_cols)
    values = projected[:, 2].astype(jnp.bfloat16).reshape(tok_rows, head_cols)
    pairs = jnp.stack([keys, values], axis=1)
    query_heads = jnp.transpose(query, (1, 0, 2))
    scale = HD ** (-0.5)
    slot_count = page_table.shape[0]
    page_start = page_table * PAGE
    page_block = page_start // half
    page_inner = page_start % half
    page_row = jnp.where(
        page_block < blocks,
        page_block * tok_rows + page_inner,
        (2 * blocks - 1 - page_block) * tok_rows + half + page_inner,
    )

    def attend_block(state, piece_block, visible):
        run_max, run_sum, run_acc = state
        keys_block = piece_block[:, 0].reshape(-1, local_heads, HD)
        values_block = piece_block[:, 1].reshape(-1, local_heads, HD)
        scores = (
            jnp.einsum("hqd,khd->hqk", query_heads, keys_block, preferred_element_type=jnp.float32)
            * scale
        )
        scores = jnp.where(visible[None], scores, NEG)
        new_max = jnp.maximum(run_max, jnp.max(scores, axis=2))
        weights = jnp.where(visible[None], jnp.exp(scores - new_max[:, :, None]), 0.0)
        factor = jnp.exp(run_max - new_max)
        new_sum = run_sum * factor + jnp.sum(weights, axis=2)
        new_acc = run_acc * factor[:, :, None] + jnp.einsum(
            "hqk,khd->hqd",
            weights.astype(jnp.bfloat16),
            values_block,
            preferred_element_type=jnp.float32,
        )
        return (new_max, new_sum, new_acc)

    piece = lax.all_gather(pairs, "blk", axis=0, tiled=True)
    start = jnp.int32(0)
    run_max = jnp.full((local_heads, tok_rows), NEG, jnp.float32)
    run_sum = jnp.zeros((local_heads, tok_rows), jnp.float32)
    run_acc = jnp.zeros((local_heads, tok_rows, HD), jnp.float32)
    cache = jnp.zeros((slot_count, PAGE, 2, head_cols), jnp.bfloat16)
    count = piece.shape[0]
    step = math.gcd(count, 1024)

    def one_step(index, state):
        begin = index * step
        piece_block = lax.dynamic_slice_in_dim(piece, begin, step, 0)
        key_rows = begin + jnp.arange(step, dtype=jnp.int32)
        key_pos = row_positions(key_rows, tok_rows, blocks)
        key_prompt, key_shift = tenant_info(key_pos, prompt_lengths)
        visible = (own_prompt[:, None] == key_prompt[None, :]) & (
            key_pos[None, :] <= own_pos[:, None]
        )
        return attend_block(state, piece_block, visible)

    run_max, run_sum, run_acc = lax.fori_loop(
        0, count // step, one_step, (run_max, run_sum, run_acc)
    )
    inside = (page_row >= start) & (page_row + PAGE <= start + count)
    offset = jnp.clip(page_row, 0, count - PAGE)

    def take_page(first):
        return lax.dynamic_slice_in_dim(piece, first, PAGE, 0)

    found = jax.vmap(take_page)(offset)
    cache = jnp.where(inside[:, None, None, None], found, cache)
    run_max, run_sum, run_acc, cache = (run_max, run_sum, run_acc, cache)
    heads_out = jnp.transpose(
        (run_acc / run_sum[:, :, None]).astype(jnp.bfloat16), (1, 0, 2)
    ).reshape(tok_rows, head_cols)
    kv_cache = jnp.transpose(cache, (0, 2, 1, 3))
    partial_value = jnp.dot(heads_out, w_o, preferred_element_type=jnp.float32)
    attended = lax.psum_scatter(
        partial_value.astype(jnp.bfloat16), "mp", scatter_dimension=0, tiled=True
    ).astype(jnp.float32)
    per_dev = tok_rows // shares
    mine = lax.dynamic_slice_in_dim(tokens, share_id * per_dev, per_dev, 0)
    residual = mine.astype(jnp.float32) + attended
    moe_in = rms_scale(residual, moe_gain).astype(jnp.bfloat16)
    local_experts = w_gate_up.shape[0]
    experts = local_experts * blocks
    cap_slots = 5 * per_dev * TOP // (3 * experts)
    total_cols = experts * cap_slots
    flat_ids = expert_ids.reshape(-1)
    onehot = (flat_ids[:, None] == jnp.arange(experts, dtype=jnp.int32)[None, :]).astype(jnp.int32)
    rank = jnp.sum((jnp.cumsum(onehot, axis=0) - onehot) * onehot, axis=1)
    column = (
        flat_ids % local_experts * (blocks * cap_slots)
        + flat_ids // local_experts * cap_slots
        + rank
    )
    select = (
        (column[:, None] == jnp.arange(total_cols, dtype=jnp.int32)[None, :])
        .astype(jnp.float32)
        .reshape(per_dev, TOP, total_cols)
    )
    spread = jnp.sum(select, axis=1).astype(jnp.bfloat16)
    mixing = jnp.einsum("rk,rkc->rc", gate_weights.astype(jnp.float32), select).astype(jnp.bfloat16)
    outgoing = lax.dot_general(
        spread, moe_in, (((0,), (0,)), ((), ())), preferred_element_type=jnp.float32
    ).astype(jnp.bfloat16)
    outgoing = outgoing.reshape(local_experts, blocks, cap_slots, width)
    gate_up = w_gate_up.reshape(local_experts, width, -1)
    ff_local = w_down.shape[1]
    copies = jnp.broadcast_to(
        outgoing[:, :, None], (local_experts, blocks, shares, cap_slots, width)
    ).reshape(local_experts, blocks * shares, cap_slots, width)
    arrived = lax.all_to_all(copies, ("blk", "mp"), split_axis=1, concat_axis=1, tiled=True)
    both = jnp.einsum(
        "end,edf->enf",
        arrived.reshape(local_experts, blocks * shares * cap_slots, width),
        gate_up,
        preferred_element_type=jnp.float32,
    )
    hidden = (jax.nn.silu(both[..., :ff_local]) * both[..., ff_local:]).astype(jnp.bfloat16)
    partial_out = jnp.einsum(
        "enf,efd->end", hidden, w_down, preferred_element_type=jnp.float32
    ).astype(jnp.bfloat16)
    partial_out = partial_out.reshape(local_experts, blocks * shares, cap_slots, width)
    returned = lax.all_to_all(partial_out, ("blk", "mp"), split_axis=1, concat_axis=1, tiled=True)
    expert_out = jnp.sum(
        returned.reshape(local_experts, blocks, shares, cap_slots, width).astype(jnp.float32),
        axis=2,
    ).astype(jnp.bfloat16)
    combined = jnp.dot(
        mixing, expert_out.reshape(total_cols, width), preferred_element_type=jnp.float32
    )
    mixed = (residual + combined).astype(jnp.bfloat16)
    return (mixed, kv_cache)


def solution(mesh):
    in_specs = (
        P("blk", None),
        P(),
        P(None, None, "mp"),
        P("mp", None),
        P(),
        P("blk", None, None, "mp"),
        P("blk", "mp", None),
        P(("blk", "mp"), None),
        P(("blk", "mp"), None),
        P(),
        P("blk"),
    )
    out_specs = (P(("blk", "mp"), None), P("blk", None, None, "mp"))
    return jax.shard_map(body, mesh=mesh, in_specs=in_specs, out_specs=out_specs, check_vma=False)
```

profile of v0, /device:TPU:10, one launch (start us, length us, event | category | flops | bytes accessed | tf_op | source)
XLA Modules:
  0.0 1270.6 jit_solution(2636821197596443969)
XLA Ops:
  8.8 33.5 %copy.108 = bf16[2048,3,2048]{0,2,1:T(8,128)(2,1)} copy(bf16[2048,3,2048]{2,0,1:T(8,128)(2,1)} %param.15) | data formatting | bytes 50331648 | tf_op args[2]
  42.2 12.3 fusion.31
  62.1 18.1 %reduce-window.22 = s32[64,12,128]{2,1,0:T(8,128)S(1)} reduce-window(s32[64,12,128]{2,1,0:T(8,128)S(1)} %fusion.37, s32[]{:T(128)} %copy.168), window={size=1x1x128 pad=0_0x0_0x127_0}, to_apply=%region_9.10 | reduce-window | flops 12484608 | bytes 786436 | tf_op jit(solution)/shard_map/reduce-window.1
  86.4 332.0 %all-gather.2.cloned.1.call-done = bf16[8192,2,2048]{0,2,1:T(8,128)(2,1)} async-done(((bf16[256,2,2048]{0,2,1:T(8,128)(2,1)}), bf16[8192,2,2048]{0,2,1:T(8,128)(2,1)}) %all-gather.2.cloned.1.call-update) | async-done | bytes 67108880 | tf_op jit(solution)/shard_map/all_gather | solution.py:118
  418.4 248.6 %while.25 = (s32[]{:T(128)}, f32[16,256]{1,0:T(8,128)S(1)}, f32[16,256]{1,0:T(8,128)S(1)}, f32[16,256,128]{2,1,0:T(8,128)}, s32[256]{0:T(256)S(1)}, /*index=5*/s...) while((s32[]{:T(128)}, f32[16,256]{1,0:T(8,128)S(1)}, ...), condition=%wide.region_8.9_spmd.clone.clone, body=%wide.region_4.8_spmd.clone.sunk.clone | while | flops 2204437504 | bytes 149191920 | solution.py:138
  419.2 7.8 constant_dynamic-slice_fusion.12
  427.0 5.1 fusion.86
  432.1 4.0 fusion.87
  437.9 11.5 fusion.89
  450.0 7.8 constant_dynamic-slice_fusion.12
  457.7 5.1 fusion.86
  462.9 4.0 fusion.87
  468.7 11.9 fusion.89
  481.0 7.8 constant_dynamic-slice_fusion.12
  488.8 5.1 fusion.86
  499.8 11.9 fusion.89
  512.1 7.8 constant_dynamic-slice_fusion.12
  519.9 5.1 fusion.86
  525.1 4.0 fusion.87
  530.8 11.9 fusion.89
  543.2 7.8 constant_dynamic-slice_fusion.12
  551.0 5.1 fusion.86
  561.9 11.9 fusion.89
  574.3 7.8 constant_dynamic-slice_fusion.12
  582.1 5.1 fusion.86
  593.0 11.9 fusion.89
  605.4 7.8 constant_dynamic-slice_fusion.12
  613.1 5.1 fusion.86
  624.1 11.9 fusion.89
  636.4 7.8 constant_dynamic-slice_fusion.12
  644.2 5.1 fusion.86
  655.2 11.9 fusion.89
  669.3 5.9 multiply_reduce_fusion
  675.3 6.2 convolution_convert_fusion
  681.5 10.1 copy.116
  691.6 6.2 all-to-all-start
  697.8 49.0 %reshape.437 = bf16[2,2048,2816]{2,1,0:T(8,128)(2,1)} reshape(bf16[2,2048,2,1408]{3,2,1,0:T(2,128)(2,1)} %param.18) | data formatting | bytes 46137344 | tf_op jit(solution)/shard_map/reshape | solution.py:185
  746.9 176.7 %all-to-all-done = bf16[2,32,40,2048]{3,2,0,1:T(8,128)(2,1)} async-done(((bf16[2,32,40,2048]{3,2,0,1:T(8,128)(2,1)}), bf16[2,32,40,2048]{3,2,0,1:T(8,128)(2,1)}, u32[]{:S(2)}, u32[]{:S(2)}) %all-to-all-start) | async-done | bytes 10485792 | tf_op jit(solution)/shard_map/all_to_all | solution.py:190
  923.6 10.1 copy.117
  933.7 38.4 %fusion.53 = f32[2,1280,2816]{2,1,0:T(8,128)} fusion(bf16[2,1280,2048]{2,1,0:T(8,128)(2,1)} %bitcast.129, bf16[2,2048,2816]{2,1,0:T(8,128)(2,1)} %reshape.437), kind=kOutput, calls=%fused_computation.134 | convolution fusion | flops 29527900160 | bytes 62390272 | tf_op jit(solution)/shard_map/end,edf->enf/dot_general | solution.py:191
  972.1 26.2 %convolution_convert_fusion.1 = bf16[2,1280,2048]{2,1,0:T(8,128)(2,1)} fusion(bf16[2,1408,2048]{2,1,0:T(8,128)(2,1)} %param.19, f32[2,1280,2816]{2,1,0:T(8,128)} %fusion.53), kind=kOutput, calls=%fused_computation.51 | convolution fusion | flops 14790819840 | bytes 50855936 | tf_op jit(solution)/shard_map/enf,efd->end/dot_general | solution.py:198
  998.3 10.1 copy.118
  1008.4 10.5 all-to-all-start.1
  1023.1 11.5 fusion.20
  1034.6 8.9 while.24
  1046.7 198.0 %all-to-all-done.1 = bf16[2,32,40,2048]{3,2,0,1:T(8,128)(2,1)} async-done(((bf16[2,32,40,2048]{3,2,0,1:T(8,128)(2,1)}), bf16[2,32,40,2048]{3,2,0,1:T(8,128)(2,1)}, u32[]{:S(2)}, u32[]{:S(2)}) %all-to-all-start.1) | async-done | bytes 10485792 | tf_op jit(solution)/shard_map/all_to_all | solution.py:202
  1244.7 10.2 copy.119
  1254.9 8.6 fusion.24
  (170 shorter events, 71.3 us)
Async XLA Ops:
  7.2 411.3 %all-gather.2.cloned.1.call-start = ((), (), s32[]{:S(2)}) async-start(), calls=%async_computation.2 | async-start | bytes 69206016 | tf_op jit(solution)/shard_map/all_gather | solution.py:118
  8.7 33.5 %copy-start.4 = (bf16[256,2048]{1,0:T(8,128)(2,1)S(1)}, bf16[256,2048]{1,0:T(8,128)(2,1)}, u32[]{:S(2)}) copy-start(bf16[256,2048]{1,0:T(8,128)(2,1)} %param.13) | copy-start | bytes 3145732
  8.8 33.5 %copy-start.13 = (f32[2048]{0:T(1024)S(1)}, f32[2048]{0:T(1024)}, u32[]{:S(2)}) copy-start(f32[2048]{0:T(1024)} %param.14) | copy-start | bytes 24580
  54.7 1.6 copy-start.14
  60.0 1.6 copy-start.10
  61.6 19.9 %copy-start.6 = (bf16[256,16,64]{0,2,1:T(8,128)(2,1)S(1)}, bf16[256,16,64]{0,2,1:T(8,128)(2,1)}, u32[]{:S(2)}) copy-start(bf16[256,16,64]{0,2,1:T(8,128)(2,1)} %get-tuple-element.425) | copy-start | bytes 1572868
  61.6 19.9 %copy-start.7 = (bf16[256,16,64]{0,2,1:T(8,128)(2,1)S(1)}, bf16[256,16,64]{0,2,1:T(8,128)(2,1)}, u32[]{:S(2)}) copy-start(bf16[256,16,64]{0,2,1:T(8,128)(2,1)} %get-tuple-element.426) | copy-start | bytes 1572868
  82.9 335.5 %copy-start.8 = (s32[256,6]{0,1:T(8,128)}, s32[256,6]{0,1:T(8,128)S(1)}, u32[]{:S(2)}) copy-start(s32[256,6]{0,1:T(8,128)S(1)} %fusion.43) | copy-start | bytes 18436
  432.1 5.8 copy-start
  462.9 5.8 copy-start
  494.0 5.8 copy-start
  525.0 5.8 copy-start
  556.1 5.8 copy-start
  587.2 5.8 copy-start
  618.3 5.8 copy-start
  649.4 5.8 copy-start
  667.0 2.2 copy-start.5
  669.3 6.0 copy-start.3
  669.3 6.0 copy-start.11
  675.3 6.3 copy-start.1
  691.6 232.0 %all-to-all-start = ((bf16[2,32,40,2048]{3,2,0,1:T(8,128)(2,1)}), bf16[2,32,40,2048]{3,2,0,1:T(8,128)(2,1)}, u32[]{:S(2)}, u32[]{:S(2)}) async-start(bf16[2,32,40,2048]{3,2,0,1:T(8,128)(2,1)} %copy.116), calls=%async_computation | async-start | bytes 20971520 | tf_op jit(solution)/shard_map/all_to_all | solution.py:190
  1008.4 10.5 copy-start.15
  1008.4 10.7 copy-start.12
  1008.4 10.9 copy-start.9
  1008.4 236.3 %all-to-all-start.1 = ((bf16[2,32,40,2048]{3,2,0,1:T(8,128)(2,1)}), bf16[2,32,40,2048]{3,2,0,1:T(8,128)(2,1)}, u32[]{:S(2)}, u32[]{:S(2)}) async-start(bf16[2,32,40,2048]{3,2,0,1:T(8,128)(2,1)} %copy.118), calls=%async_computation.1 | async-start | bytes 20971520 | tf_op jit(solution)/shard_map/all_to_all | solution.py:202
  1046.7 208.2 %copy-start.2 = (f32[256,2048]{1,0:T(8,128)S(1)}, f32[256,2048]{1,0:T(8,128)}, u32[]{:S(2)}) copy-start(f32[256,2048]{1,0:T(8,128)} %copy-done.1) | copy-start | bytes 6291460
Sparse Core Ops, SparseCore 0:
  61.7 356.6 all-gather.1
where the time goes:
time: 1290 us; the launch traced here: 1270 us
  waiting for transfers between devices  707 us (55%)
  matrix products  245 us (19%)
  local copies, waits for them, and re-layouts  214 us (17%)
  other arithmetic  72.2 us (6%)
  starting transfers between devices  16.7 us (1%)
  between operations  14.6 us (1%)
    all_gather x1, waiting for transfers between devices, body(): piece = lax.all_gather(pairs, 'blk', axis=0, tiled=True)  332 us
    all_to_all x1, waiting for transfers between devices, body(): lax.all_to_all(partial_out, ('blk', 'mp'), split_axis=1, concat_axis=1, t...  198 us
    all_to_all x1, waiting for transfers between devices, body(): lax.all_to_all(copies, ('blk', 'mp'), split_axis=1, concat_axis=1, tiled=...  177 us
    dot_general x8, matrix products, attend_block(): jnp.einsum('hqk,khd->hqd', weights.astype(jnp.bfloat16), values_block, pr...  94.7 us
    slice x8, local copies, waits for them, and re-layouts, attend_block(): values_block = piece_block[:, 1].reshape(-1, local_heads, HD)  62.3 us
    reshape x1, local copies, waits for them, and re-layouts, body(): gate_up = w_gate_up.reshape(local_experts, width, -1)  49 us
    dot_general x8, matrix products, attend_block(): jnp.einsum('hqd,khd->hqk', query_heads, keys_block, preferred_element_typ...  41 us
    dot_general x1, matrix products, body(): jnp.einsum('end,edf->enf', arrived.reshape(local_experts, blocks * shares...  38.4 us
  transfers between devices with their start and end apart: 3, of which 3 were waited for; matrix products, arithmetic and copies ran while one was open for 8% of the time, Pallas kernels for 0%

commit v1 on v0

--- a/solution.py
+++ b/solution.py
@@ -3,6 +3,8 @@
 import jax
 import jax.numpy as jnp
 from jax import lax
+from jax.experimental import pallas as pl
+from jax.experimental.pallas import tpu as pltpu
 from jax.sharding import PartitionSpec as P
 
 HD = 128
@@ -50,7 +52,7 @@
     return (prompt, positions - begin)
 
 
-def body(
+def gathered_body(
     tokens,
     attn_gain,
     w_qkv,
@@ -211,6 +213,298 @@
     return (mixed, kv_cache)
 
 
+Q_BLOCKS = 2
+K_STEP = 512
+PLANE = 8
+
+
+def attend_kernel(
+    info, pages, q_ref, k_own, k_other, v_own, v_other, out_ref, cache_ref, k_all, v_all, top, total, acc
+):
+    sources, half, _ = q_ref.shape
+    count = 2 * sources
+    core = info[0]
+
+    def source(block):
+        return jnp.where(block < sources, block, count - 1 - block)
+
+    def arrange(index, _):
+        mine = 2 * index + core
+        theirs = 2 * index + 1 - core
+        at_mine = pl.ds(pl.multiple_of(mine * half, half), half)
+        at_theirs = pl.ds(pl.multiple_of(theirs * half, half), half)
+        k_all[at_mine] = k_own[source(mine)]
+        v_all[at_mine] = v_own[source(mine)]
+        k_all[at_theirs] = k_other[source(theirs)]
+        v_all[at_theirs] = v_other[source(theirs)]
+        return 0
+
+    lax.fori_loop(0, sources, arrange, 0)
+
+    def store_page(index, _):
+        at_page = pl.ds(pl.multiple_of(pages[index] * PAGE, PAGE), PAGE)
+        cache_ref[index, 0] = k_all[at_page]
+        cache_ref[index, 1] = v_all[at_page]
+        return 0
+
+    lax.fori_loop(0, cache_ref.shape[0], store_page, 0)
+
+    rows = Q_BLOCKS * half
+    factor = HD ** (-0.5) * math.log2(math.e)
+    tenants = info.shape[0] - 1
+
+    def begin_of(position):
+        begin = jnp.zeros_like(position)
+        for tenant in range(1, tenants):
+            start = info[1 + tenant]
+            begin = jnp.where(position >= start, start, begin)
+        return begin
+
+    def one_group(group, _):
+        first_block = 2 * Q_BLOCKS * group + core
+        query = jnp.concatenate(
+            [q_ref[source(first_block + 2 * i)] for i in range(Q_BLOCKS)], axis=0
+        )
+        row = lax.broadcasted_iota(jnp.int32, (rows, 1), 0)
+        q_pos = first_block * half + row + row // half * half
+        begin = begin_of(q_pos)
+        first = first_block * half
+        last = first + (2 * Q_BLOCKS - 1) * half - 1
+        k_first = begin_of(first) // K_STEP
+        k_end = last // K_STEP + 1
+        full_from = jnp.minimum((begin_of(last) + K_STEP - 1) // K_STEP, k_end)
+        full_to = jnp.maximum(full_from, (first + 1) // K_STEP)
+        top[...] = jnp.full_like(top, NEG)
+        total[...] = jnp.zeros_like(total)
+        acc[...] = jnp.zeros_like(acc)
+
+        def step(masked):
+            def run(index, _):
+                at = pl.ds(pl.multiple_of(index * K_STEP, K_STEP), K_STEP)
+                scores = lax.dot_general(
+                    query, k_all[at], (((1,), (1,)), ((), ())), preferred_element_type=jnp.float32
+                )
+                if masked:
+                    k_pos = index * K_STEP + lax.broadcasted_iota(jnp.int32, (rows, K_STEP), 1)
+                    scores = jnp.where((k_pos >= begin) & (k_pos <= q_pos), scores, NEG)
+                old = top[...]
+                new = jnp.maximum(old, jnp.max(scores, axis=1, keepdims=True))
+                weights = jnp.exp2((scores - new[:, :1]) * factor)
+                shrink = jnp.exp2((old - new) * factor)
+                sums = weights[:, :128]
+                for part in range(1, K_STEP // 128):
+                    sums = sums + weights[:, part * 128 : (part + 1) * 128]
+                total[...] = total[...] * shrink + sums
+                acc[...] = acc[...] * shrink + jnp.dot(
+                    weights.astype(jnp.bfloat16), v_all[at], preferred_element_type=jnp.float32
+                )
+                top[...] = new
+                return 0
+
+            return run
+
+        lax.fori_loop(k_first, full_from, step(True), 0)
+        lax.fori_loop(full_from, full_to, step(False), 0)
+        lax.fori_loop(full_to, k_end, step(True), 0)
+        heads = (acc[...] / jnp.sum(total[...], axis=1, keepdims=True)).astype(jnp.bfloat16)
+        for i in range(Q_BLOCKS):
+            out_ref[source(first_block + 2 * i)] = heads[i * half : (i + 1) * half]
+        return 0
+
+    lax.fori_loop(0, sources // Q_BLOCKS, one_group, 0)
+
+
+def attend(info, pages, query, k_own, k_other, v_own, v_other):
+    sources, half, _ = query.shape
+    slots = pages.shape[0]
+    rows = Q_BLOCKS * half
+    positions = 2 * sources * half
+    vmem = pl.BlockSpec(memory_space=pltpu.VMEM)
+    smem = pl.BlockSpec(memory_space=pltpu.SMEM)
+    return pl.pallas_call(
+        attend_kernel,
+        out_shape=(
+            jax.ShapeDtypeStruct((sources, half, HD), jnp.bfloat16),
+            jax.ShapeDtypeStruct((slots, 2, PAGE, HD), jnp.bfloat16),
+        ),
+        in_specs=[smem, smem] + [vmem] * 5,
+        out_specs=(vmem, vmem),
+        scratch_shapes=[
+            pltpu.VMEM((positions, HD), jnp.bfloat16),
+            pltpu.VMEM((positions, HD), jnp.bfloat16),
+            pltpu.VMEM((rows, 128), jnp.float32),
+            pltpu.VMEM((rows, 128), jnp.float32),
+            pltpu.VMEM((rows, HD), jnp.float32),
+        ],
+        compiler_params=pltpu.CompilerParams(vmem_limit_bytes=32 * 2**20),
+        cost_estimate=pl.CostEstimate(
+            flops=2 * 10**10, bytes_accessed=10**7, transcendentals=10**7
+        ),
+    )(info, pages, query, k_own, k_other, v_own, v_other)
+
+
+def routed_body(
+    tokens,
+    attn_gain,
+    w_qkv,
+    w_o,
+    moe_gain,
+    w_gate_up,
+    w_down,
+    expert_ids,
+    gate_weights,
+    prompt_lengths,
+    page_table,
+):
+    blocks = lax.axis_size("blk")
+    block_id = lax.axis_index("blk")
+    rows, width = tokens.shape
+    half = rows // 2
+    heads = w_qkv.shape[2] // HD
+    core = block_id % 2
+    planes = blocks // PLANE
+    plane_id = block_id // PLANE
+    experts_here = w_gate_up.shape[0]
+    ff = w_down.shape[1]
+    plane_groups = [[z * PLANE + p for p in range(PLANE)] for z in range(planes)]
+    line_groups = [[z * PLANE + p for z in range(planes)] for p in range(PLANE)]
+
+    own_rows = block_id * rows + jnp.arange(rows, dtype=jnp.int32)
+    own_pos = row_positions(own_rows, rows, blocks)
+    _, relative = tenant_info(own_pos, prompt_lengths)
+    normed = rms_scale(tokens.astype(jnp.float32), attn_gain).astype(jnp.bfloat16)
+
+    def project(part):
+        return jnp.dot(normed, w_qkv[:, part], preferred_element_type=jnp.float32).reshape(
+            rows, heads, HD
+        )
+
+    def by_head(values):
+        cut = jnp.transpose(values.reshape(2, half, heads, HD), (2, 0, 1, 3))
+        cut = jnp.where(block_id % 2 == 1, cut[:, ::-1], cut)
+        return lax.all_to_all(cut.reshape(blocks, half, HD), "blk", 0, 0, tiled=True)
+
+    keys = by_head(rotate(project(1), relative).astype(jnp.bfloat16))
+    values = by_head(project(2).astype(jnp.bfloat16))
+    query = by_head(rotate(project(0), relative).astype(jnp.bfloat16))
+    swap = [(i, i ^ 1) for i in range(blocks)]
+    k_other = lax.ppermute(keys, "blk", swap)
+    v_other = lax.ppermute(values, "blk", swap)
+    all_pages = lax.all_gather(page_table, "blk", axis=0, tiled=False)
+    slots = all_pages.shape[1]
+    core_pages = jnp.where(core == 0, all_pages[:, 0::2], all_pages[:, 1::2]).reshape(-1)
+    starts = jnp.cumsum(prompt_lengths) - prompt_lengths
+    info = jnp.concatenate([core[None], starts]).astype(jnp.int32)
+    heads_out, cache = attend(info, core_pages, query, keys, k_other, values, v_other)
+    heads_out = lax.all_to_all(heads_out, "blk", 0, 0, tiled=True).reshape(heads, 2, half, HD)
+    heads_out = jnp.where(block_id % 2 == 1, heads_out[:, ::-1], heads_out)
+    heads_out = jnp.transpose(heads_out, (1, 2, 0, 3)).reshape(rows, heads * HD)
+
+    attended = jnp.dot(heads_out, w_o, preferred_element_type=jnp.float32)
+    residual = tokens.astype(jnp.float32) + attended
+    moe_in = rms_scale(residual, moe_gain).astype(jnp.bfloat16)
+
+    experts = experts_here * blocks
+    cap = 5 * rows * TOP // (3 * experts)
+    plane_experts = experts_here * PLANE
+    plane_slots = plane_experts * cap
+    routing = lax.all_gather(
+        jnp.concatenate([expert_ids.astype(jnp.bfloat16), gate_weights], axis=1),
+        "blk",
+        axis=0,
+        tiled=False,
+        axis_index_groups=line_groups,
+    )
+    named = (
+        routing[:, :, :TOP, None].astype(jnp.int32)
+        == plane_id * plane_experts + jnp.arange(plane_experts, dtype=jnp.int32)
+    )
+    weight = jnp.sum(jnp.where(named, routing[:, :, TOP:, None].astype(jnp.float32), 0.0), axis=2)
+    named = jnp.any(named, axis=2)
+    before = jnp.tril(jnp.ones((rows, rows), jnp.bfloat16), -1)
+    rank = jnp.einsum(
+        "ts,zse->zte", before, named.astype(jnp.bfloat16), preferred_element_type=jnp.float32
+    )
+    rank = jnp.where(named, rank, -1.0).astype(jnp.bfloat16)
+    slot = jnp.arange(plane_slots, dtype=jnp.int32)
+    widen = (slot[None, :] // cap == jnp.arange(plane_experts, dtype=jnp.int32)[:, None]).astype(
+        jnp.bfloat16
+    )
+    chosen = (
+        jnp.einsum("zte,es->zts", rank, widen, preferred_element_type=jnp.float32)
+        == (slot % cap).astype(jnp.float32)
+    )
+    mixing = jnp.where(
+        chosen,
+        jnp.einsum(
+            "zte,es->zts", weight.astype(jnp.bfloat16), widen, preferred_element_type=jnp.float32
+        ),
+        0.0,
+    ).astype(jnp.bfloat16)
+    chosen = chosen.astype(jnp.bfloat16)
+    gate_up = jnp.transpose(w_gate_up, (0, 2, 1, 3))
+
+    def to_plane(shift, rows_in):
+        source = (plane_id + shift) % planes
+        pick = lax.dynamic_index_in_dim(chosen, source, 0, keepdims=False)
+        outgoing = lax.dot_general(
+            pick, rows_in, (((0,), (0,)), ((), ())), preferred_element_type=jnp.float32
+        ).astype(jnp.bfloat16)
+        return lax.all_to_all(
+            outgoing.reshape(PLANE, experts_here, cap, width),
+            "blk",
+            0,
+            0,
+            tiled=True,
+            axis_index_groups=plane_groups,
+        )
+
+    def run_experts(arrived):
+        inputs = jnp.transpose(arrived, (1, 0, 2, 3)).reshape(experts_here, PLANE * cap, width)
+        gate = jnp.einsum("end,edf->enf", inputs, gate_up[:, 0], preferred_element_type=jnp.float32)
+        up = jnp.einsum("end,edf->enf", inputs, gate_up[:, 1], preferred_element_type=jnp.float32)
+        hidden = (jax.nn.silu(gate) * up).astype(jnp.bfloat16)
+        out = jnp.einsum(
+            "enf,efd->end", hidden, w_down, preferred_element_type=jnp.float32
+        ).astype(jnp.bfloat16)
+        return jnp.transpose(out.reshape(experts_here, PLANE, cap, width), (1, 0, 2, 3))
+
+    def from_plane(shift, out):
+        source = (plane_id + shift) % planes
+        returned = lax.all_to_all(
+            out, "blk", 0, 0, tiled=True, axis_index_groups=plane_groups
+        ).reshape(plane_slots, width)
+        mix = lax.dynamic_index_in_dim(mixing, source, 0, keepdims=False)
+        return jnp.dot(mix, returned, preferred_element_type=jnp.float32)
+
+    def along_line(values, shift):
+        return lax.ppermute(
+            values, "blk", [(i, (i + shift * PLANE) % blocks) for i in range(blocks)]
+        )
+
+    order = [0, 1, 3, 2]
+    inputs = {s: moe_in if s == 0 else along_line(moe_in, -s) for s in order}
+    outs = {s: run_experts(to_plane(s, inputs[s])) for s in order}
+    mixed = residual
+    for s in [1, 3, 2, 0]:
+        part = from_plane(s, outs[s])
+        if s != 0:
+            part = along_line(part.astype(jnp.bfloat16), s).astype(jnp.float32)
+        mixed = mixed + part
+
+    cache = lax.all_to_all(
+        cache.reshape(blocks, slots // 2, 2, PAGE, HD), "blk", 0, 0, tiled=True
+    ).reshape(heads, 2, slots // 2, 2, PAGE, HD)
+    kv_cache = jnp.transpose(cache, (2, 1, 3, 4, 0, 5)).reshape(slots, 2, PAGE, heads * HD)
+    return (mixed.astype(jnp.bfloat16), kv_cache)
+
+
+def body(*args):
+    heads = args[2].shape[2] // HD
+    by_head = lax.axis_size("mp") == 1 and 2 * heads == lax.axis_size("blk")
+    return routed_body(*args) if by_head else gathered_body(*args)
+
+
 def solution(mesh):
     in_specs = (
         P("blk", None),

time: 1290 us -> 749 us (0.58); the launches traced: 1270 us -> 743 us
  waiting for transfers between devices: 707 us -> 197 us
  blocking collectives: 0 us -> 128 us
  local copies, waits for them, and re-layouts: 214 us -> 123 us
  matrix products: 245 us -> 167 us
  other arithmetic: 72.2 us -> 8.73 us
  starting transfers between devices: 16.7 us -> 71.2 us
  Pallas kernels: 0 us -> 46.4 us
    all_gather x1 -> x0, waiting for transfers between devices: 332 us -> none  [body(): piece = lax.all_gather(pairs, 'blk', axis=0, tiled=True)]
    all_to_all x2 -> x12, waiting for transfers between devices: 375 us -> 69.1 us  [the longest x3 40.1 us: by_head(): lax.all_to_all(cut.reshape(blocks, half, HD), 'blk', 0, 0, tiled=True)]
    ppermute x0 -> x8, waiting for transfers between devices: none -> 128 us  [the longest x6 128 us: along_line(): lax.ppermute(values, 'blk', [(i, (i + shift * PLANE) % blocks) for i in r...]
    dot_general x23 -> x26, matrix products: 245 us -> 167 us  [the longest x4 44 us: run_experts(): jnp.einsum('end,edf->enf', inputs, gate_up[:, 1], preferred_element_type=...]
    slice x9 -> x1, local copies, waits for them, and re-layouts: 62.4 us -> 0.01 us  [routed_body(): routing[:, :, TOP:, None].astype(jnp.float32)]
    dot_general x0 -> x4, local copies, waits for them, and re-layouts: none -> 54 us  [project(): jnp.dot(normed, w_qkv[:, part], preferred_element_type=jnp.float32)]
    all_gather x0 -> x1, blocking collectives: none -> 53 us  [routed_body(): lax.all_gather(jnp.concatenate([expert_ids.astype(jnp.bfloat16), gate_wei...]
    pallas_call x0 -> x1, Pallas kernels: none -> 46.4 us  [attend(): pl.pallas_call(attend_kernel, out_shape=(jax.ShapeDtypeStruct((sources, h...]
  transfers between devices with their start and end apart: 3 -> 20, of which waited for: 3 -> 11; matrix products, arithmetic and copies ran while one was open for 8% -> 28% of each run, Pallas kernels for 0% -> 0%
where the time goes in v1:
time: 749 us; the launch traced here: 743 us
  waiting for transfers between devices  197 us (26%)
  matrix products  167 us (22%)
  blocking collectives  128 us (17%)
  local copies, waits for them, and re-layouts  123 us (16%)
  starting transfers between devices  71.2 us (10%)
  Pallas kernels  46.4 us (6%)
  other arithmetic  8.73 us (1%)
    ppermute x6, waiting for transfers between devices, along_line(): lax.ppermute(values, 'blk', [(i, (i + shift * PLANE) % blocks) for i in r...  128 us
    dot_general x4, local copies, waits for them, and re-layouts, project(): jnp.dot(normed, w_qkv[:, part], preferred_element_type=jnp.float32)  54 us
    all_gather x1, blocking collectives, routed_body(): lax.all_gather(jnp.concatenate([expert_ids.astype(jnp.bfloat16), gate_wei...  53 us
    pallas_call x1, Pallas kernels, attend(): pl.pallas_call(attend_kernel, out_shape=(jax.ShapeDtypeStruct((sources, h...  46.4 us
    unnamed x1, blocking collectives  44.7 us
    dot_general x4, matrix products, run_experts(): jnp.einsum('end,edf->enf', inputs, gate_up[:, 1], preferred_element_type=...  44 us
    all_to_all x3, waiting for transfers between devices, by_head(): lax.all_to_all(cut.reshape(blocks, half, HD), 'blk', 0, 0, tiled=True)  40.1 us
    dot_general x4, matrix products, run_experts(): jnp.einsum('enf,efd->end', hidden, w_down, preferred_element_type=jnp.flo...  36.2 us
  transfers between devices with their start and end apart: 20, of which 11 were waited for; matrix products, arithmetic and copies ran while one was open for 28% of the time, Pallas kernels for 0%

profile of v1, /device:TPU:10, one launch (start us, length us, event | category | flops | bytes accessed | tf_op | source)
XLA Modules:
  0.0 743.1 jit_solution(18387983783418487373)
XLA Ops:
  2.1 16.9 %slice_bitcast_fusion.2 = (bf16[2048,2048]{0,1:T(8,128)(2,1)}, bf16[2048,2048]{0,1:T(8,128)(2,1)}, bf16[2048,2048]{0,1:T(8,128)(2,1)}) fusion(bf16[2048,3,2048]{2,0,1:T(8,128)(2,1)} %param.13), kind=kLoop, calls=%fused_computation.3 | loop fusion | bytes 50331648 | tf_op jit(solution)/shard_map/dot_general | solution.py:378
  19.0 12.4 %copy.83 = bf16[2048,2048]{1,0:T(8,128)(2,1)} copy(bf16[2048,2048]{0,1:T(8,128)(2,1)} %get-tuple-element.8) | data formatting | bytes 16777216 | tf_op jit(solution)/shard_map/dot_general | solution.py:378
  31.9 12.4 %copy.79 = bf16[2048,2048]{1,0:T(8,128)(2,1)} copy(bf16[2048,2048]{0,1:T(8,128)(2,1)} %get-tuple-element.7) | data formatting | bytes 16777216 | tf_op jit(solution)/shard_map/dot_general | solution.py:378
  44.3 6.0 fusion.55
  54.1 12.4 %copy.87 = bf16[2048,2048]{1,0:T(8,128)(2,1)} copy(bf16[2048,2048]{0,1:T(8,128)(2,1)} %get-tuple-element.6) | data formatting | bytes 16777216 | tf_op jit(solution)/shard_map/dot_general | solution.py:378
  66.4 5.2 convolution_convert_fusion.11
  81.4 6.0 all-to-all-start.1
  88.7 23.5 %all-to-all-done.1.k_own = bf16[32,128,128]{2,1,0:T(8,128)(2,1)S(1)} async-done(((bf16[32,128,128]{2,1,0:T(8,128)(2,1)}), bf16[32,128,128]{2,1,0:T(8,128)(2,1)S(1)}, u32[]{:S(2)}, u32[]{:S(2)}) %all-to-all-start.1) | async-done | bytes 1048608 | tf_op jit(solution)/shard_map/all_to_all | solution.py:385
  112.2 5.1 all-to-all-start.2
  125.5 16.6 %all-to-all-done.2.v_own = bf16[32,128,128]{2,1,0:T(8,128)(2,1)S(1)} async-done(((bf16[32,128,128]{2,1,0:T(8,128)(2,1)}), bf16[32,128,128]{2,1,0:T(8,128)(2,1)S(1)}, u32[]{:S(2)}, u32[]{:S(2)}) %all-to-all-start.2) | async-done | bytes 1048608 | tf_op jit(solution)/shard_map/all_to_all | solution.py:385
  142.1 5.1 all-to-all-start
  148.0 44.7 %all-reduce = s32[64]{0:T(128)S(1)} all-reduce(s32[64]{0:T(128)S(1)} %dynamic-update-slice), channel_id=2, replica_groups=mesh['blk'=32,'mp'=1] {'blk'}, use_global_device_ids=true, to_apply=%add | all-reduce | flops 64 | bytes 512
  193.0 46.4 %shard_map.122 = (bf16[32,128,128]{2,1,0:T(8,128)(2,1)S(1)}, bf16[32,2,128,128]{3,2,1,0:T(8,128)(2,1)}) custom-call(s32[5]{0:T(128)S(1)} %pad_add_fusion.info, s32[32]{0:T(128)S(1)} %fusion.66.pages, bf16[32,128,128]{2,1,0:T(8,128)(2,1)S(1)} %all-to-all-done.q_ref, bf16[32,128,128]{2,1,0:T(8,128)(2,1)S(1)} %all-to-all-done.1.k_own, ...), custom_call_target="tpu_custom_call" | custom-call | flops 20000000000 | bytes 10000000 | tf_op jit(solution)/shard_map/pallas_call | solution.py:324
  239.5 30.0 %all_to_all.65 = bf16[32,128,128]{2,1,0:T(8,128)(2,1)S(1)} all-to-all(bf16[32,128,128]{2,1,0:T(8,128)(2,1)S(1)} %get-tuple-element.4), channel_id=1, replica_groups=mesh['blk'=32,'mp'=1] {'blk'}, dimensions={0} | all-to-all | bytes 2097152 | tf_op jit(solution)/shard_map/all_to_all | solution.py:399
  269.5 5.1 all-to-all-start.12
  274.7 53.0 %all-gather.1 = bf16[1024,12]{0,1:T(8,128)(2,1)S(1)} all-gather(bf16[256,12]{0,1:T(8,128)(2,1)S(1)} %pad_maximum_fusion), channel_id=3, replica_groups={{0,8,16,24},{1,9,17,25},{2,10,18,26},{3,11,19,27},{4,12,20,28},{5,13,21..., dimensions={0}, use_global_device_ids=true | all-gather | bytes 30720 | tf_op jit(solution)/shard_map/all_gather | solution.py:411
  332.1 5.9 multiply_reduce_fusion
  344.0 4.2 all-to-all-start.10
  350.6 45.1 %collective-permute-done.6 = bf16[256,2048]{1,0:T(8,128)(2,1)} collective-permute-done((bf16[256,2048]{1,0:T(8,128)(2,1)}, bf16[256,2048]{1,0:T(8,128)(2,1)}, u32[]{:S(2)}, u32[]{:S(2)}) %collective-permute-start.6) | collective-permute-done | bytes 1048608 | tf_op jit(solution)/shard_map/ppermute | solution.py:481
  399.3 4.6 all-to-all-start.8
  406.8 21.9 %copy.126 = bf16[2,2048,2,1408]{3,1,0,2:T(8,128)(2,1)} copy(bf16[2,2048,2,1408]{3,2,1,0:T(2,128)(2,1)} %param.16) | data formatting | bytes 46137344 | tf_op args[5]
  434.8 6.3 all-to-all-start.6
  441.1 12.8 %collective-permute-done.2 = bf16[256,2048]{1,0:T(8,128)(2,1)} collective-permute-done((bf16[256,2048]{1,0:T(8,128)(2,1)}, bf16[256,2048]{1,0:T(8,128)(2,1)}, u32[]{:S(2)}, u32[]{:S(2)}) %collective-permute-start.2) | collective-permute-done | bytes 1048608 | tf_op jit(solution)/shard_map/ppermute | solution.py:481
  459.1 11.7 %fusion = f32[2,320,1408]{2,1,0:T(8,128)} fusion(bf16[2,320,2048]{2,1,0:T(8,128)(2,1)} %bitcast.226, bf16[2,2,2048,1408]{3,2,0,1:T(8,128)(2,1)} %bitcast.193), kind=kOutput, calls=%fused_computation.6 | convolution fusion | flops 3690987520 | bytes 17760256 | tf_op jit(solution)/shard_map/end,edf->enf/dot_general | solution.py:464
  474.6 7.9 %fusion.1 = f32[2,320,1408]{2,1,0:T(8,128)} fusion(bf16[2,320,2048]{2,1,0:T(8,128)(2,1)} %bitcast.228, bf16[2,2,2048,1408]{3,2,0,1:T(8,128)(2,1)S(1)} %bitcast.200), kind=kOutput, calls=%fused_computation.7 | convolution fusion | flops 3690987520 | bytes 17760256 | tf_op jit(solution)/shard_map/end,edf->enf/dot_general | solution.py:464
  482.5 4.9 all-to-all-start.4
  487.4 11.7 %fusion.13 = bf16[2,320,1408]{2,1,0:T(8,128)(2,1)} fusion(bf16[2,320,2048]{2,1,0:T(8,128)(2,1)} %bitcast.229, bf16[2,2,2048,1408]{3,2,0,1:T(8,128)(2,1)} %bitcast.194, f32[2,320,1408]{2,1,0:T(8,128)} %fusion.1), kind=kOutput, calls=%fused_computation.19 | convolution fusion | flops 3696394240 | bytes 19562496 | tf_op jit(solution)/shard_map/end,edf->enf/dot_general | solution.py:465
  499.1 9.2 %convolution_convert_fusion.2 = bf16[2,320,2048]{2,1,0:T(8,128)(2,1)S(1)} fusion(bf16[2,320,1408]{2,1,0:T(8,128)(2,1)} %fusion.13, bf16[2,1408,2048]{2,1,0:T(8,128)(2,1)} %param.17), kind=kOutput, calls=%fused_computation.24 | convolution fusion | flops 3692298240 | bytes 15958016 | tf_op jit(solution)/shard_map/enf,efd->end/dot_general | solution.py:467
  513.8 7.9 %fusion.2 = f32[2,320,1408]{2,1,0:T(8,128)} fusion(bf16[2,320,2048]{2,1,0:T(8,128)(2,1)} %bitcast.230, bf16[2,2,2048,1408]{3,2,0,1:T(8,128)(2,1)S(1)} %bitcast.203), kind=kOutput, calls=%fused_computation.8 | convolution fusion | flops 3690987520 | bytes 17760256 | tf_op jit(solution)/shard_map/end,edf->enf/dot_general | solution.py:464
  521.7 4.6 all-to-all-start.9
  526.3 11.7 %fusion.14 = bf16[2,320,1408]{2,1,0:T(8,128)(2,1)} fusion(bf16[2,320,2048]{2,1,0:T(8,128)(2,1)} %bitcast.231, bf16[2,2,2048,1408]{3,2,0,1:T(8,128)(2,1)} %bitcast.195, f32[2,320,1408]{2,1,0:T(8,128)} %fusion.2), kind=kOutput, calls=%fused_computation.20 | convolution fusion | flops 3696394240 | bytes 19562496 | tf_op jit(solution)/shard_map/end,edf->enf/dot_general | solution.py:465
  538.0 9.2 %convolution_convert_fusion.4 = bf16[2,320,2048]{2,1,0:T(8,128)(2,1)S(1)} fusion(bf16[2,320,1408]{2,1,0:T(8,128)(2,1)} %fusion.14, bf16[2,1408,2048]{2,1,0:T(8,128)(2,1)} %param.17), kind=kOutput, calls=%fused_computation.26 | convolution fusion | flops 3692298240 | bytes 15958016 | tf_op jit(solution)/shard_map/enf,efd->end/dot_general | solution.py:467
  552.7 7.9 %fusion.3 = f32[2,320,1408]{2,1,0:T(8,128)} fusion(bf16[2,320,2048]{2,1,0:T(8,128)(2,1)} %bitcast.232, bf16[2,2,2048,1408]{3,2,0,1:T(8,128)(2,1)S(1)} %bitcast.206), kind=kOutput, calls=%fused_computation.9 | convolution fusion | flops 3690987520 | bytes 17760256 | tf_op jit(solution)/shard_map/end,edf->enf/dot_general | solution.py:464
  560.6 4.5 all-to-all-start.7
  565.1 10.4 %fusion.15 = bf16[2,320,1408]{2,1,0:T(8,128)(2,1)S(1)} fusion(bf16[2,320,2048]{2,1,0:T(8,128)(2,1)} %bitcast.233, bf16[2,2,2048,1408]{3,2,0,1:T(8,128)(2,1)} %bitcast.196, f32[2,320,1408]{2,1,0:T(8,128)} %fusion.3), kind=kOutput, calls=%fused_computation.21 | convolution fusion | flops 3696394240 | bytes 19562496 | tf_op jit(solution)/shard_map/end,edf->enf/dot_general | solution.py:465
  575.5 8.9 %convolution_convert_fusion.6 = bf16[2,320,2048]{2,1,0:T(8,128)(2,1)S(1)} fusion(bf16[2,320,1408]{2,1,0:T(8,128)(2,1)S(1)} %fusion.15, bf16[2,1408,2048]{2,1,0:T(8,128)(2,1)} %param.17), kind=kOutput, calls=%fused_computation.28 | convolution fusion | flops 3692298240 | bytes 15958016 | tf_op jit(solution)/shard_map/enf,efd->end/dot_general | solution.py:467
  586.2 9.6 %all-to-all-done.7 = bf16[8,2,40,2048]{3,2,1,0:T(8,128)(2,1)S(1)} async-done(((bf16[8,2,40,2048]{3,2,1,0:T(8,128)(2,1)}), bf16[8,2,40,2048]{3,2,1,0:T(8,128)(2,1)S(1)}, u32[]{:S(2)}, u32[]{:S(2)}) %all-to-all-start.7) | async-done | bytes 2621472 | tf_op jit(solution)/shard_map/all_to_all | solution.py:474
  597.3 5.8 all-to-all-start.5
  603.1 10.3 %fusion.12 = bf16[2,320,1408]{2,1,0:T(8,128)(2,1)S(1)} fusion(bf16[2,320,2048]{2,1,0:T(8,128)(2,1)} %bitcast.227, bf16[2,2,2048,1408]{3,2,0,1:T(8,128)(2,1)} %bitcast.197, f32[2,320,1408]{2,1,0:T(8,128)} %fusion), kind=kOutput, calls=%fused_computation.18 | convolution fusion | flops 3696394240 | bytes 19562496 | tf_op jit(solution)/shard_map/end,edf->enf/dot_general | solution.py:465
  613.4 8.9 %convolution_convert_fusion = bf16[2,320,2048]{2,1,0:T(8,128)(2,1)S(1)} fusion(bf16[2,320,1408]{2,1,0:T(8,128)(2,1)S(1)} %fusion.12, bf16[2,1408,2048]{2,1,0:T(8,128)(2,1)} %param.17), kind=kOutput, calls=%fused_computation.22 | convolution fusion | flops 3692298240 | bytes 15958016 | tf_op jit(solution)/shard_map/enf,efd->end/dot_general | solution.py:467
  624.1 9.9 %all-to-all-done.5 = bf16[8,2,40,2048]{3,2,1,0:T(8,128)(2,1)} async-done(((bf16[8,2,40,2048]{3,2,1,0:T(8,128)(2,1)}), bf16[8,2,40,2048]{3,2,1,0:T(8,128)(2,1)}, u32[]{:S(2)}, u32[]{:S(2)}) %all-to-all-start.5) | async-done | bytes 2621472 | tf_op jit(solution)/shard_map/all_to_all | solution.py:474
  634.0 5.5 all-to-all-start.11
  640.2 4.4 convolution_convert_fusion.8
  656.6 4.2 reshape.308
  660.7 9.5 %all-to-all-done.11 = bf16[8,2,40,2048]{3,2,1,0:T(8,128)(2,1)S(1)} async-done(((bf16[8,2,40,2048]{3,2,1,0:T(8,128)(2,1)}), bf16[8,2,40,2048]{3,2,1,0:T(8,128)(2,1)S(1)}, u32[]{:S(2)}, u32[]{:S(2)}) %all-to-all-start.11) | async-done | bytes 2621472 | tf_op jit(solution)/shard_map/all_to_all | solution.py:474
  670.2 44.8 %collective-permute-done.7 = bf16[256,2048]{1,0:T(8,128)(2,1)} collective-permute-done((bf16[256,2048]{1,0:T(8,128)(2,1)}, bf16[256,2048]{1,0:T(8,128)(2,1)}, u32[]{:S(2)}, u32[]{:S(2)}) %collective-permute-start.7) | collective-permute-done | bytes 1048608 | tf_op jit(solution)/shard_map/ppermute | solution.py:481
  715.0 23.0 %collective-permute-done.5 = bf16[256,2048]{1,0:T(8,128)(2,1)} collective-permute-done((bf16[256,2048]{1,0:T(8,128)(2,1)}, bf16[256,2048]{1,0:T(8,128)(2,1)}, u32[]{:S(2)}, u32[]{:S(2)}) %collective-permute-start.5) | collective-permute-done | bytes 1048608 | tf_op jit(solution)/shard_map/ppermute | solution.py:481
  738.0 4.6 add_convert_fusion
  (167 shorter events, 88.7 us)
Async XLA Ops:
  19.0 12.4 %copy-start.11 = (bf16[256,2048]{1,0:T(8,128)(2,1)S(1)}, bf16[256,2048]{1,0:T(8,128)(2,1)}, u32[]{:S(2)}) copy-start(bf16[256,2048]{1,0:T(8,128)(2,1)} %param.11) | copy-start | bytes 3145732
  31.9 12.4 %copy-start.23 = (f32[2048]{0:T(1024)S(1)}, f32[2048]{0:T(1024)}, u32[]{:S(2)}) copy-start(f32[2048]{0:T(1024)} %param.12) | copy-start | bytes 24580
  44.3 6.0 copy-start.2
  81.4 30.8 %all-to-all-start.1 = ((bf16[32,128,128]{2,1,0:T(8,128)(2,1)}), bf16[32,128,128]{2,1,0:T(8,128)(2,1)S(1)}, u32[]{:S(2)}, u32[]{:S(2)}) async-start(bf16[32,128,128]{2,1,0:T(8,128)(2,1)} %bitcast.17), calls=%async_computation.1 | async-start | bytes 2097152 | tf_op jit(solution)/shard_map/all_to_all | solution.py:385
  112.2 29.9 %all-to-all-start.2 = ((bf16[32,128,128]{2,1,0:T(8,128)(2,1)}), bf16[32,128,128]{2,1,0:T(8,128)(2,1)S(1)}, u32[]{:S(2)}, u32[]{:S(2)}) async-start(bf16[32,128,128]{2,1,0:T(8,128)(2,1)} %bitcast.23), calls=%async_computation.2 | async-start | bytes 2097152 | tf_op jit(solution)/shard_map/all_to_all | solution.py:385
  124.2 23.5 %copy-start.24 = (s32[2]{0:T(128)S(1)}, s32[2]{0:T(128)}, u32[]{:S(2)}) copy-start(s32[2]{0:T(128)} %param.21) | copy-start | bytes 28
  142.1 50.9 %all-to-all-start = ((bf16[32,128,128]{2,1,0:T(8,128)(2,1)}), bf16[32,128,128]{2,1,0:T(8,128)(2,1)S(1)}, u32[]{:S(2)}, u32[]{:S(2)}) async-start(bf16[32,128,128]{2,1,0:T(8,128)(2,1)} %bitcast.225), calls=%async_computation | async-start | bytes 2097152 | tf_op jit(solution)/shard_map/all_to_all | solution.py:385
  147.2 45.8 %collective-permute-start = (bf16[32,128,128]{2,1,0:T(8,128)(2,1)S(1)}, bf16[32,128,128]{2,1,0:T(8,128)(2,1)}, u32[]{:S(2)}, u32[]{:S(2)}) collective-permute-start(bf16[32,128,128]{2,1,0:T(8,128)(2,1)S(1)} %all-to-all-done.1.k_own), channel_id=1, source_target_pairs={{0,1},{1,0},{2,3},{3,2},{4,5},{5,4},{6,7},{7,6},{8,9},{9,8},{10,11... | collective-permute-start | bytes 3145736 | tf_op jit(solution)/shard_map/ppermute | solution.py:391
  147.4 45.6 %collective-permute-start.1 = (bf16[32,128,128]{2,1,0:T(8,128)(2,1)S(1)}, bf16[32,128,128]{2,1,0:T(8,128)(2,1)}, u32[]{:S(2)}, u32[]{:S(2)}) collective-permute-start(bf16[32,128,128]{2,1,0:T(8,128)(2,1)S(1)} %all-to-all-done.2.v_own), channel_id=1, source_target_pairs={{0,1},{1,0},{2,3},{3,2},{4,5},{5,4},{6,7},{7,6},{8,9},{9,8},{10,11... | collective-permute-start | bytes 3145736 | tf_op jit(solution)/shard_map/ppermute | solution.py:392
  269.5 73.2 %all-to-all-start.12 = ((bf16[32,1,2,128,128]{4,3,2,1,0:T(8,128)(2,1)}), bf16[32,1,2,128,128]{4,3,2,1,0:T(8,128)(2,1)S(1)}, u32[]{:S(2)}, u32[]{:S(2)}) async-start(bf16[32,1,2,128,128]{4,3,2,1,0:T(8,128)(2,1)} %bitcast.65), calls=%async_computation.12 | async-start | bytes 4194304 | tf_op jit(solution)/shard_map/all_to_all | solution.py:495
  332.1 5.9 copy-start.18
  344.0 55.2 %all-to-all-start.10 = ((bf16[8,2,40,2048]{3,2,1,0:T(8,128)(2,1)}), bf16[8,2,40,2048]{3,2,1,0:T(8,128)(2,1)S(1)}, u32[]{:S(2)}, u32[]{:S(2)}) async-start(bf16[8,2,40,2048]{3,2,1,0:T(8,128)(2,1)} %bitcast.58), calls=%async_computation.10 | async-start | bytes 5242880 | tf_op jit(solution)/shard_map/all_to_all | solution.py:453
  348.2 47.5 %collective-permute-start.6 = (bf16[256,2048]{1,0:T(8,128)(2,1)}, bf16[256,2048]{1,0:T(8,128)(2,1)}, u32[]{:S(2)}, u32[]{:S(2)}) collective-permute-start(bf16[256,2048]{1,0:T(8,128)(2,1)} %copy-done.7), channel_id=1, source_target_pairs={{0,16},{1,17},{2,18},{3,19},{4,20},{5,21},{6,22},{7,23},{8,24},{9,... | collective-permute-start | bytes 3145736 | tf_op jit(solution)/shard_map/ppermute | solution.py:481
  399.3 35.5 %all-to-all-start.8 = ((bf16[8,2,40,2048]{3,2,1,0:T(8,128)(2,1)}), bf16[8,2,40,2048]{3,2,1,0:T(8,128)(2,1)}, u32[]{:S(2)}, u32[]{:S(2)}) async-start(bf16[8,2,40,2048]{3,2,1,0:T(8,128)(2,1)} %bitcast.50), calls=%async_computation.8 | async-start | bytes 5242880 | tf_op jit(solution)/shard_map/all_to_all | solution.py:453
  403.9 27.1 %collective-permute-start.4 = (bf16[256,2048]{1,0:T(8,128)(2,1)}, bf16[256,2048]{1,0:T(8,128)(2,1)}, u32[]{:S(2)}, u32[]{:S(2)}) collective-permute-start(bf16[256,2048]{1,0:T(8,128)(2,1)} %copy-done.7), channel_id=1, source_target_pairs={{0,8},{1,9},{2,10},{3,11},{4,12},{5,13},{6,14},{7,15},{8,16},{9,17... | collective-permute-start | bytes 3145736 | tf_op jit(solution)/shard_map/ppermute | solution.py:481
  404.9 49.0 %collective-permute-start.2 = (bf16[256,2048]{1,0:T(8,128)(2,1)}, bf16[256,2048]{1,0:T(8,128)(2,1)}, u32[]{:S(2)}, u32[]{:S(2)}) collective-permute-start(bf16[256,2048]{1,0:T(8,128)(2,1)} %copy-done.7), channel_id=1, source_target_pairs={{0,24},{1,25},{2,26},{3,27},{4,28},{5,29},{6,30},{7,31},{8,0},{9,1... | collective-permute-start | bytes 3145736 | tf_op jit(solution)/shard_map/ppermute | solution.py:481
  434.8 47.7 %all-to-all-start.6 = ((bf16[8,2,40,2048]{3,2,1,0:T(8,128)(2,1)}), bf16[8,2,40,2048]{3,2,1,0:T(8,128)(2,1)}, u32[]{:S(2)}, u32[]{:S(2)}) async-start(bf16[8,2,40,2048]{3,2,1,0:T(8,128)(2,1)} %bitcast.42), calls=%async_computation.6 | async-start | bytes 5242880 | tf_op jit(solution)/shard_map/all_to_all | solution.py:453
  457.4 17.1 %slice-start = ((s8[23068672]{0:T(1024)(128)(4,1)}), s8[4194304]{0:T(1024)(128)(4,1)S(1)}, s32[]{:S(2)}) async-start(s8[23068672]{0:T(1024)(128)(4,1)} %bitcast.198), calls=%async_computation.13 | async-start | bytes 8388608
  459.1 15.4 %slice-start.1 = ((s8[23068672]{0:T(1024)(128)(4,1)}), s8[4194304]{0:T(1024)(128)(4,1)S(1)}, s32[]{:S(2)}) async-start(s8[23068672]{0:T(1024)(128)(4,1)} %bitcast.198), calls=%async_computation.14 | async-start | bytes 8388608
  459.1 15.4 %slice-start.2 = ((s8[23068672]{0:T(1024)(128)(4,1)}), s8[4194304]{0:T(1024)(128)(4,1)S(1)}, s32[]{:S(2)}) async-start(s8[23068672]{0:T(1024)(128)(4,1)} %bitcast.198), calls=%async_computation.15 | async-start | bytes 8388608
  459.1 15.4 %slice-start.3 = ((s8[23068672]{0:T(1024)(128)(4,1)}), s8[4194304]{0:T(1024)(128)(4,1)S(1)}, s32[]{:S(2)}) async-start(s8[23068672]{0:T(1024)(128)(4,1)} %bitcast.198), calls=%async_computation.16 | async-start | bytes 8388608
  459.1 15.4 %slice-start.4 = ((s8[23068672]{0:T(1024)(128)(4,1)}), s8[4194304]{0:T(1024)(128)(4,1)S(1)}, s32[]{:S(2)}) async-start(s8[23068672]{0:T(1024)(128)(4,1)} %bitcast.198), calls=%async_computation.17 | async-start | bytes 8388608
  459.1 15.4 %slice-start.5 = ((s8[23068672]{0:T(1024)(128)(4,1)}), s8[2097152]{0:T(1024)(128)(4,1)S(1)}, s32[]{:S(2)}) async-start(s8[23068672]{0:T(1024)(128)(4,1)} %bitcast.198), calls=%async_computation.18 | async-start | bytes 4194304
  482.5 39.2 %all-to-all-start.4 = ((bf16[8,2,40,2048]{3,2,1,0:T(8,128)(2,1)}), bf16[8,2,40,2048]{3,2,1,0:T(8,128)(2,1)}, u32[]{:S(2)}, u32[]{:S(2)}) async-start(bf16[8,2,40,2048]{3,2,1,0:T(8,128)(2,1)} %bitcast.207), calls=%async_computation.4 | async-start | bytes 5242880 | tf_op jit(solution)/shard_map/all_to_all | solution.py:453
  487.3 26.4 %slice-start.6 = ((s8[23068672]{0:T(1024)(128)(4,1)}), s8[2097152]{0:T(1024)(128)(4,1)S(1)}, s32[]{:S(2)}) async-start(s8[23068672]{0:T(1024)(128)(4,1)} %bitcast.201), calls=%async_computation.19 | async-start | bytes 4194304
  487.3 26.4 %slice-start.7 = ((s8[23068672]{0:T(1024)(128)(4,1)}), s8[4194304]{0:T(1024)(128)(4,1)S(1)}, s32[]{:S(2)}) async-start(s8[23068672]{0:T(1024)(128)(4,1)} %bitcast.201), calls=%async_computation.20 | async-start | bytes 8388608
  487.4 26.4 %slice-start.8 = ((s8[23068672]{0:T(1024)(128)(4,1)}), s8[4194304]{0:T(1024)(128)(4,1)S(1)}, s32[]{:S(2)}) async-start(s8[23068672]{0:T(1024)(128)(4,1)} %bitcast.201), calls=%async_computation.21 | async-start | bytes 8388608
  487.4 26.4 %slice-start.9 = ((s8[23068672]{0:T(1024)(128)(4,1)}), s8[4194304]{0:T(1024)(128)(4,1)S(1)}, s32[]{:S(2)}) async-start(s8[23068672]{0:T(1024)(128)(4,1)} %bitcast.201), calls=%async_computation.22 | async-start | bytes 8388608
  499.1 14.7 %slice-start.10 = ((s8[23068672]{0:T(1024)(128)(4,1)}), s8[4194304]{0:T(1024)(128)(4,1)S(1)}, s32[]{:S(2)}) async-start(s8[23068672]{0:T(1024)(128)(4,1)} %bitcast.201), calls=%async_computation.23 | async-start | bytes 8388608
  499.1 14.7 %slice-start.11 = ((s8[23068672]{0:T(1024)(128)(4,1)}), s8[4194304]{0:T(1024)(128)(4,1)S(1)}, s32[]{:S(2)}) async-start(s8[23068672]{0:T(1024)(128)(4,1)} %bitcast.201), calls=%async_computation.24 | async-start | bytes 8388608
  521.7 38.9 %all-to-all-start.9 = ((bf16[8,2,40,2048]{3,2,1,0:T(8,128)(2,1)}), bf16[8,2,40,2048]{3,2,1,0:T(8,128)(2,1)}, u32[]{:S(2)}, u32[]{:S(2)}) async-start(bf16[8,2,40,2048]{3,2,1,0:T(8,128)(2,1)} %bitcast.212), calls=%async_computation.9 | async-start | bytes 5242880 | tf_op jit(solution)/shard_map/all_to_all | solution.py:474
  526.3 26.3 %slice-start.12 = ((s8[23068672]{0:T(1024)(128)(4,1)}), s8[2097152]{0:T(1024)(128)(4,1)S(1)}, s32[]{:S(2)}) async-start(s8[23068672]{0:T(1024)(128)(4,1)} %bitcast.204), calls=%async_computation.25 | async-start | bytes 4194304
  526.3 26.3 %slice-start.13 = ((s8[23068672]{0:T(1024)(128)(4,1)}), s8[4194304]{0:T(1024)(128)(4,1)S(1)}, s32[]{:S(2)}) async-start(s8[23068672]{0:T(1024)(128)(4,1)} %bitcast.204), calls=%async_computation.26 | async-start | bytes 8388608
  526.3 26.3 %slice-start.14 = ((s8[23068672]{0:T(1024)(128)(4,1)}), s8[4194304]{0:T(1024)(128)(4,1)S(1)}, s32[]{:S(2)}) async-start(s8[23068672]{0:T(1024)(128)(4,1)} %bitcast.204), calls=%async_computation.27 | async-start | bytes 8388608
  526.3 26.3 %slice-start.15 = ((s8[23068672]{0:T(1024)(128)(4,1)}), s8[4194304]{0:T(1024)(128)(4,1)S(1)}, s32[]{:S(2)}) async-start(s8[23068672]{0:T(1024)(128)(4,1)} %bitcast.204), calls=%async_computation.28 | async-start | bytes 8388608
  538.0 14.6 %slice-start.16 = ((s8[23068672]{0:T(1024)(128)(4,1)}), s8[4194304]{0:T(1024)(128)(4,1)S(1)}, s32[]{:S(2)}) async-start(s8[23068672]{0:T(1024)(128)(4,1)} %bitcast.204), calls=%async_computation.29 | async-start | bytes 8388608
  538.0 14.6 %slice-start.17 = ((s8[23068672]{0:T(1024)(128)(4,1)}), s8[4194304]{0:T(1024)(128)(4,1)S(1)}, s32[]{:S(2)}) async-start(s8[23068672]{0:T(1024)(128)(4,1)} %bitcast.204), calls=%async_computation.30 | async-start | bytes 8388608
  560.6 35.2 %all-to-all-start.7 = ((bf16[8,2,40,2048]{3,2,1,0:T(8,128)(2,1)}), bf16[8,2,40,2048]{3,2,1,0:T(8,128)(2,1)S(1)}, u32[]{:S(2)}, u32[]{:S(2)}) async-start(bf16[8,2,40,2048]{3,2,1,0:T(8,128)(2,1)} %bitcast.213), calls=%async_computation.7 | async-start | bytes 5242880 | tf_op jit(solution)/shard_map/all_to_all | solution.py:474
  597.3 36.7 %all-to-all-start.5 = ((bf16[8,2,40,2048]{3,2,1,0:T(8,128)(2,1)}), bf16[8,2,40,2048]{3,2,1,0:T(8,128)(2,1)}, u32[]{:S(2)}, u32[]{:S(2)}) async-start(bf16[8,2,40,2048]{3,2,1,0:T(8,128)(2,1)} %bitcast.214), calls=%async_computation.5 | async-start | bytes 5242880 | tf_op jit(solution)/shard_map/all_to_all | solution.py:474
  634.0 5.7 copy-start.9
  634.0 5.7 copy-start.17
  634.0 36.3 %all-to-all-start.11 = ((bf16[8,2,40,2048]{3,2,1,0:T(8,128)(2,1)}), bf16[8,2,40,2048]{3,2,1,0:T(8,128)(2,1)S(1)}, u32[]{:S(2)}, u32[]{:S(2)}) async-start(bf16[8,2,40,2048]{3,2,1,0:T(8,128)(2,1)} %bitcast.211), calls=%async_computation.11 | async-start | bytes 5242880 | tf_op jit(solution)/shard_map/all_to_all | solution.py:474
  639.7 6.5 copy-start.1
  640.2 9.7 %copy-start.6 = (bf16[4,256,640]{2,1,0:T(8,128)(2,1)}, bf16[4,256,640]{2,1,0:T(8,128)(2,1)S(1)}, u32[]{:S(2)}) copy-start(bf16[4,256,640]{2,1,0:T(8,128)(2,1)S(1)} %select_convert_fusion) | copy-start | bytes 3932164
  644.6 70.4 %collective-permute-start.7 = (bf16[256,2048]{1,0:T(8,128)(2,1)}, bf16[256,2048]{1,0:T(8,128)(2,1)}, u32[]{:S(2)}, u32[]{:S(2)}) collective-permute-start(bf16[256,2048]{1,0:T(8,128)(2,1)} %convolution_convert_fusion.8), channel_id=1, source_target_pairs={{0,16},{1,17},{2,18},{3,19},{4,20},{5,21},{6,22},{7,23},{8,24},{9,... | collective-permute-start | bytes 3145736 | tf_op jit(solution)/shard_map/ppermute | solution.py:481
  648.1 5.8 copy-start.4
  648.1 89.8 %collective-permute-start.5 = (bf16[256,2048]{1,0:T(8,128)(2,1)}, bf16[256,2048]{1,0:T(8,128)(2,1)}, u32[]{:S(2)}, u32[]{:S(2)}) collective-permute-start(bf16[256,2048]{1,0:T(8,128)(2,1)} %convolution_convert_fusion.9), channel_id=1, source_target_pairs={{0,24},{1,25},{2,26},{3,27},{4,28},{5,29},{6,30},{7,31},{8,0},{9,1... | collective-permute-start | bytes 3145736 | tf_op jit(solution)/shard_map/ppermute | solution.py:481
  653.7 84.3 %collective-permute-start.3 = (bf16[256,2048]{1,0:T(8,128)(2,1)}, bf16[256,2048]{1,0:T(8,128)(2,1)}, u32[]{:S(2)}, u32[]{:S(2)}) collective-permute-start(bf16[256,2048]{1,0:T(8,128)(2,1)} %convolution_convert_fusion.10), channel_id=1, source_target_pairs={{0,8},{1,9},{2,10},{3,11},{4,12},{5,13},{6,14},{7,15},{8,16},{9,17... | collective-permute-start | bytes 3145736 | tf_op jit(solution)/shard_map/ppermute | solution.py:481
  (15 other events, 42.3 us)

commit v2 on v1

--- a/solution.py
+++ b/solution.py
@@ -1,3 +1,4 @@
+import functools
 import math
 
 import jax
@@ -213,41 +214,116 @@
     return (mixed, kv_cache)
 
 
-Q_BLOCKS = 2
-K_STEP = 512
+Q_BLOCKS = 4
+K_STEP = 1024
 PLANE = 8
-
-
-def attend_kernel(
-    info, pages, q_ref, k_own, k_other, v_own, v_other, out_ref, cache_ref, k_all, v_all, top, total, acc
-):
+VMEM_BYTES = 56 * 2**20
+
+
+def project_kernel(turned, flip, x_ref, w_ref, cos_ref, sin_ref, out_ref):
+    rows = x_ref.shape[0]
+    half = rows // 2
+    projected = jnp.dot(x_ref[...], w_ref[0], preferred_element_type=jnp.float32)
+    for head in range(out_ref.shape[0]):
+        part = projected[:, head * HD : (head + 1) * HD]
+        if turned:
+            part = part * cos_ref[...] + pltpu.roll(part, HD // 2, 1) * sin_ref[...]
+        part = part.astype(jnp.bfloat16)
+        out_ref[head, flip[0]] = part[:half]
+        out_ref[head, 1 - flip[0]] = part[half:]
+
+
+def project(normed, weights, part, flip, cosine, sine, turned):
+    rows, width = normed.shape
+    heads = weights.shape[2] // HD
+    group = 4
+    return pl.pallas_call(
+        functools.partial(project_kernel, turned),
+        grid=(heads // group,),
+        in_specs=[
+            pl.BlockSpec(memory_space=pltpu.SMEM),
+            pl.BlockSpec((rows, width), lambda i: (0, 0)),
+            pl.BlockSpec((1, width, group * HD), lambda i: (part, 0, i)),
+            pl.BlockSpec((rows, HD), lambda i: (0, 0)),
+            pl.BlockSpec((rows, HD), lambda i: (0, 0)),
+        ],
+        out_specs=pl.BlockSpec((group, 2, rows // 2, HD), lambda i: (i, 0, 0, 0)),
+        out_shape=jax.ShapeDtypeStruct((heads, 2, rows // 2, HD), jnp.bfloat16),
+        compiler_params=pltpu.CompilerParams(vmem_limit_bytes=32 * 2**20),
+        cost_estimate=pl.CostEstimate(
+            flops=2 * rows * width * heads * HD, bytes_accessed=2 * width * heads * HD, transcendentals=0
+        ),
+    )(flip, normed, weights, cosine, sine)
+
+
+def cache_kernel(info, pages, k_own, k_other, v_own, v_other, out_ref, sems):
+    sources = k_own.shape[0]
+    core = info[0]
+
+    def copy(index, ref, which):
+        page = pages[index]
+        held = jnp.where(page < sources, page, 2 * sources - 1 - page)
+        return pltpu.make_async_copy(ref.at[held], out_ref.at[index, which], sems.at[index, which])
+
+    def start(index, _):
+        mine = (pages[index] + core) % 2 == 0
+
+        @pl.when(mine)
+        def _():
+            copy(index, k_own, 0).start()
+            copy(index, v_own, 1).start()
+
+        @pl.when(jnp.logical_not(mine))
+        def _():
+            copy(index, k_other, 0).start()
+            copy(index, v_other, 1).start()
+
+        return 0
+
+    def finish(index, _):
+        copy(index, k_own, 0).wait()
+        copy(index, v_own, 1).wait()
+        return 0
+
+    lax.fori_loop(0, out_ref.shape[0], start, 0)
+    lax.fori_loop(0, out_ref.shape[0], finish, 0)
+
+
+def cache_pages(info, pages, k_own, k_other, v_own, v_other):
+    smem = pl.BlockSpec(memory_space=pltpu.SMEM)
+    anywhere = pl.BlockSpec(memory_space=pl.ANY)
+    count = pages.shape[0]
+    return pl.pallas_call(
+        cache_kernel,
+        out_shape=jax.ShapeDtypeStruct((count, 2) + k_own.shape[1:], jnp.bfloat16),
+        in_specs=[smem, smem] + [anywhere] * 4,
+        out_specs=anywhere,
+        scratch_shapes=[pltpu.SemaphoreType.DMA((count, 2))],
+        cost_estimate=pl.CostEstimate(flops=0, bytes_accessed=4 * k_own.size * 2, transcendentals=0),
+    )(info, pages, k_own, k_other, v_own, v_other)
+
+
+def attend_kernel(info, q_ref, k_own, k_other, v_own, v_other, out_ref, k_all, v_all, top, total, acc):
     sources, half, _ = q_ref.shape
     count = 2 * sources
     core = info[0]
+    per_step = K_STEP // half
 
     def source(block):
         return jnp.where(block < sources, block, count - 1 - block)
 
     def arrange(index, _):
-        mine = 2 * index + core
-        theirs = 2 * index + 1 - core
-        at_mine = pl.ds(pl.multiple_of(mine * half, half), half)
-        at_theirs = pl.ds(pl.multiple_of(theirs * half, half), half)
-        k_all[at_mine] = k_own[source(mine)]
-        v_all[at_mine] = v_own[source(mine)]
-        k_all[at_theirs] = k_other[source(theirs)]
-        v_all[at_theirs] = v_other[source(theirs)]
+        for part in range(per_step):
+            block = index * per_step + part
+            held = source(block)
+            mine = (block + core) % 2 == 0
+            k_block = jnp.where(mine, k_own[held], k_other[held])
+            v_block = jnp.where(mine, v_own[held], v_other[held])
+            k_all[index, part * half : (part + 1) * half] = k_block
+            v_all[index, :, part * half : (part + 1) * half] = jnp.transpose(v_block)
         return 0
 
-    lax.fori_loop(0, sources, arrange, 0)
-
-    def store_page(index, _):
-        at_page = pl.ds(pl.multiple_of(pages[index] * PAGE, PAGE), PAGE)
-        cache_ref[index, 0] = k_all[at_page]
-        cache_ref[index, 1] = v_all[at_page]
-        return 0
-
-    lax.fori_loop(0, cache_ref.shape[0], store_page, 0)
+    lax.fori_loop(0, count // per_step, arrange, 0)
 
     rows = Q_BLOCKS * half
     factor = HD ** (-0.5) * math.log2(math.e)
@@ -265,7 +341,7 @@
         query = jnp.concatenate(
             [q_ref[source(first_block + 2 * i)] for i in range(Q_BLOCKS)], axis=0
         )
-        row = lax.broadcasted_iota(jnp.int32, (rows, 1), 0)
+        row = lax.broadcasted_iota(jnp.int32, (1, rows), 1)
         q_pos = first_block * half + row + row // half * half
         begin = begin_of(q_pos)
         first = first_block * half
@@ -280,23 +356,19 @@
 
         def step(masked):
             def run(index, _):
-                at = pl.ds(pl.multiple_of(index * K_STEP, K_STEP), K_STEP)
                 scores = lax.dot_general(
-                    query, k_all[at], (((1,), (1,)), ((), ())), preferred_element_type=jnp.float32
+                    k_all[index], query, (((1,), (1,)), ((), ())), preferred_element_type=jnp.float32
                 )
                 if masked:
-                    k_pos = index * K_STEP + lax.broadcasted_iota(jnp.int32, (rows, K_STEP), 1)
+                    k_pos = index * K_STEP + lax.broadcasted_iota(jnp.int32, (K_STEP, rows), 0)
                     scores = jnp.where((k_pos >= begin) & (k_pos <= q_pos), scores, NEG)
                 old = top[...]
-                new = jnp.maximum(old, jnp.max(scores, axis=1, keepdims=True))
-                weights = jnp.exp2((scores - new[:, :1]) * factor)
+                new = jnp.maximum(old, jnp.max(scores, axis=0, keepdims=True))
+                weights = jnp.exp2((scores - new) * factor)
                 shrink = jnp.exp2((old - new) * factor)
-                sums = weights[:, :128]
-                for part in range(1, K_STEP // 128):
-                    sums = sums + weights[:, part * 128 : (part + 1) * 128]
-                total[...] = total[...] * shrink + sums
+                total[...] = total[...] * shrink + jnp.sum(weights, axis=0, keepdims=True)
                 acc[...] = acc[...] * shrink + jnp.dot(
-                    weights.astype(jnp.bfloat16), v_all[at], preferred_element_type=jnp.float32
+                    v_all[index], weights.astype(jnp.bfloat16), preferred_element_type=jnp.float32
                 )
                 top[...] = new
                 return 0
@@ -306,7 +378,7 @@
         lax.fori_loop(k_first, full_from, step(True), 0)
         lax.fori_loop(full_from, full_to, step(False), 0)
         lax.fori_loop(full_to, k_end, step(True), 0)
-        heads = (acc[...] / jnp.sum(total[...], axis=1, keepdims=True)).astype(jnp.bfloat16)
+        heads = jnp.transpose(acc[...] / total[...]).astype(jnp.bfloat16)
         for i in range(Q_BLOCKS):
             out_ref[source(first_block + 2 * i)] = heads[i * half : (i + 1) * half]
         return 0
@@ -314,33 +386,145 @@
     lax.fori_loop(0, sources // Q_BLOCKS, one_group, 0)
 
 
-def attend(info, pages, query, k_own, k_other, v_own, v_other):
+def attend(info, query, k_own, k_other, v_own, v_other):
     sources, half, _ = query.shape
-    slots = pages.shape[0]
     rows = Q_BLOCKS * half
-    positions = 2 * sources * half
+    steps = 2 * sources * half // K_STEP
     vmem = pl.BlockSpec(memory_space=pltpu.VMEM)
     smem = pl.BlockSpec(memory_space=pltpu.SMEM)
     return pl.pallas_call(
         attend_kernel,
-        out_shape=(
-            jax.ShapeDtypeStruct((sources, half, HD), jnp.bfloat16),
-            jax.ShapeDtypeStruct((slots, 2, PAGE, HD), jnp.bfloat16),
-        ),
-        in_specs=[smem, smem] + [vmem] * 5,
-        out_specs=(vmem, vmem),
+        out_shape=jax.ShapeDtypeStruct((sources, half, HD), jnp.bfloat16),
+        in_specs=[smem] + [vmem] * 5,
+        out_specs=vmem,
         scratch_shapes=[
-            pltpu.VMEM((positions, HD), jnp.bfloat16),
-            pltpu.VMEM((positions, HD), jnp.bfloat16),
-            pltpu.VMEM((rows, 128), jnp.float32),
-            pltpu.VMEM((rows, 128), jnp.float32),
-            pltpu.VMEM((rows, HD), jnp.float32),
+            pltpu.VMEM((steps, K_STEP, HD), jnp.bfloat16),
+            pltpu.VMEM((steps, HD, K_STEP), jnp.bfloat16),
+            pltpu.VMEM((1, rows), jnp.float32),
+            pltpu.VMEM((1, rows), jnp.float32),
+            pltpu.VMEM((HD, rows), jnp.float32),
         ],
         compiler_params=pltpu.CompilerParams(vmem_limit_bytes=32 * 2**20),
         cost_estimate=pl.CostEstimate(
             flops=2 * 10**10, bytes_accessed=10**7, transcendentals=10**7
         ),
-    )(info, pages, query, k_own, k_other, v_own, v_other)
+    )(info, query, k_own, k_other, v_own, v_other)
+
+
+def attended_kernel(flip, heads_ref, w_ref, tokens_ref, gain_ref, residual_ref, normed_ref, joined):
+    step = pl.program_id(0)
+    heads, _, half, _ = heads_ref.shape
+    columns = w_ref.shape[1]
+
+    @pl.when(step == 0)
+    def _():
+        for head in range(heads):
+            at = slice(head * HD, (head + 1) * HD)
+            joined[:half, at] = heads_ref[head, flip[0]]
+            joined[half:, at] = heads_ref[head, 1 - flip[0]]
+
+    at = pl.ds(pl.multiple_of(step * columns, columns), columns)
+    attended = jnp.dot(joined[...], w_ref[...], preferred_element_type=jnp.float32)
+    residual_ref[:, at] = tokens_ref[:, at].astype(jnp.float32) + attended
+
+    @pl.when(step == pl.num_programs(0) - 1)
+    def _():
+        residual = residual_ref[...]
+        normed_ref[...] = rms_scale(residual, gain_ref[...]).astype(jnp.bfloat16)
+
+
+def attended_residual(flip, heads_out, w_o, tokens, gain):
+    rows, width = tokens.shape
+    columns = 512
+    whole = lambda *shape: pl.BlockSpec(shape, lambda i: (0,) * len(shape))
+    return pl.pallas_call(
+        attended_kernel,
+        grid=(width // columns,),
+        in_specs=[
+            pl.BlockSpec(memory_space=pltpu.SMEM),
+            whole(*heads_out.shape),
+            pl.BlockSpec((w_o.shape[0], columns), lambda i: (0, i)),
+            whole(rows, width),
+            whole(1, width),
+        ],
+        out_specs=(whole(rows, width), whole(rows, width)),
+        out_shape=(
+            jax.ShapeDtypeStruct((rows, width), jnp.float32),
+            jax.ShapeDtypeStruct((rows, width), jnp.bfloat16),
+        ),
+        scratch_shapes=[pltpu.VMEM((rows, w_o.shape[0]), jnp.bfloat16)],
+        compiler_params=pltpu.CompilerParams(vmem_limit_bytes=32 * 2**20),
+        cost_estimate=pl.CostEstimate(
+            flops=2 * rows * width * w_o.shape[0], bytes_accessed=2 * w_o.size, transcendentals=0
+        ),
+    )(flip, heads_out, w_o, tokens, gain[None])
+
+
+def experts_kernel(x_ref, gate_up_hbm, down_hbm, out_ref, gate_up, down, hidden, gate_up_sems, down_sems):
+    experts, tiles = gate_up.shape[:2]
+
+    def gate_up_copy(expert, tile):
+        return pltpu.make_async_copy(
+            gate_up_hbm.at[expert, tile], gate_up.at[expert, tile], gate_up_sems.at[expert, tile]
+        )
+
+    def down_copy(expert):
+        return pltpu.make_async_copy(down_hbm.at[expert], down.at[expert], down_sems.at[expert])
+
+    for expert in range(experts):
+        for tile in range(tiles):
+            gate_up_copy(expert, tile).start()
+        down_copy(expert).start()
+
+    def one_expert(expert, _):
+        def one_tile(tile, _):
+            gate_up_copy(expert, tile).wait()
+            both = jnp.dot(x_ref[expert], gate_up[expert, tile], preferred_element_type=jnp.float32)
+            gate, up = both[:, :128], both[:, 128:]
+            at = pl.ds(pl.multiple_of(tile * 128, 128), 128)
+            hidden[:, at] = (gate / (1.0 + jnp.exp(-gate)) * up).astype(jnp.bfloat16)
+            return 0
+
+        lax.fori_loop(0, tiles, one_tile, 0)
+        down_copy(expert).wait()
+
+        def one_column(column, _):
+            at = pl.ds(pl.multiple_of(column * 512, 512), 512)
+            out_ref[expert, :, at] = jnp.dot(
+                hidden[...], down[expert, :, at], preferred_element_type=jnp.float32
+            ).astype(jnp.bfloat16)
+            return 0
+
+        lax.fori_loop(0, out_ref.shape[2] // 512, one_column, 0)
+        return 0
+
+    lax.fori_loop(0, experts, one_expert, 0)
+
+
+def run_experts(inputs, gate_up, down):
+    experts, rows, width = inputs.shape
+    ff = down.shape[1]
+    vmem = pl.BlockSpec(memory_space=pltpu.VMEM)
+    anywhere = pl.BlockSpec(memory_space=pl.ANY)
+    return pl.pallas_call(
+        experts_kernel,
+        out_shape=jax.ShapeDtypeStruct((experts, rows, width), jnp.bfloat16),
+        in_specs=[vmem, anywhere, anywhere],
+        out_specs=vmem,
+        scratch_shapes=[
+            pltpu.VMEM(gate_up.shape, jnp.bfloat16),
+            pltpu.VMEM(down.shape, jnp.bfloat16),
+            pltpu.VMEM((rows, ff), jnp.bfloat16),
+            pltpu.SemaphoreType.DMA(gate_up.shape[:2]),
+            pltpu.SemaphoreType.DMA(down.shape[:1]),
+        ],
+        compiler_params=pltpu.CompilerParams(vmem_limit_bytes=VMEM_BYTES),
+        cost_estimate=pl.CostEstimate(
+            flops=6 * experts * rows * width * ff,
+            bytes_accessed=2 * (gate_up.size + down.size + 2 * inputs.size),
+            transcendentals=experts * rows * ff,
+        ),
+    )(inputs, gate_up, down)
 
 
 def routed_body(
@@ -366,60 +550,63 @@
     plane_id = block_id // PLANE
     experts_here = w_gate_up.shape[0]
     ff = w_down.shape[1]
+    slots = page_table.shape[0]
     plane_groups = [[z * PLANE + p for p in range(PLANE)] for z in range(planes)]
-    line_groups = [[z * PLANE + p for z in range(planes)] for p in range(PLANE)]
+
+    def exchange(values, groups=None):
+        return lax.all_to_all(values, "blk", 0, 0, tiled=True, axis_index_groups=groups)
+
+    def along_line(values, shift):
+        return lax.ppermute(
+            values, "blk", [(i, (i + shift * PLANE) % blocks) for i in range(blocks)]
+        )
+
+    page_rows = jnp.pad(page_table.astype(jnp.bfloat16)[None], ((0, 7), (0, 128 - slots)))
+    all_pages = exchange(jnp.broadcast_to(page_rows, (blocks, 8, 128)))[:, 0, :slots].astype(jnp.int32)
+    routing = jnp.concatenate([expert_ids.astype(jnp.bfloat16), gate_weights], axis=1)
+    routings = [routing] + [along_line(routing, -shift) for shift in range(1, planes)]
 
     own_rows = block_id * rows + jnp.arange(rows, dtype=jnp.int32)
     own_pos = row_positions(own_rows, rows, blocks)
     _, relative = tenant_info(own_pos, prompt_lengths)
     normed = rms_scale(tokens.astype(jnp.float32), attn_gain).astype(jnp.bfloat16)
-
-    def project(part):
-        return jnp.dot(normed, w_qkv[:, part], preferred_element_type=jnp.float32).reshape(
-            rows, heads, HD
-        )
-
-    def by_head(values):
-        cut = jnp.transpose(values.reshape(2, half, heads, HD), (2, 0, 1, 3))
-        cut = jnp.where(block_id % 2 == 1, cut[:, ::-1], cut)
-        return lax.all_to_all(cut.reshape(blocks, half, HD), "blk", 0, 0, tiled=True)
-
-    keys = by_head(rotate(project(1), relative).astype(jnp.bfloat16))
-    values = by_head(project(2).astype(jnp.bfloat16))
-    query = by_head(rotate(project(0), relative).astype(jnp.bfloat16))
+    inverse = THETA ** (-jnp.arange(HD // 2, dtype=jnp.float32) / (HD // 2))
+    angle = relative.astype(jnp.float32)[:, None] * inverse[None, :]
+    cosine, sine = jnp.cos(angle), jnp.sin(angle)
+    cosine = jnp.concatenate([cosine, cosine], axis=1)
+    sine = jnp.concatenate([-sine, sine], axis=1)
+    by_part = jnp.transpose(w_qkv, (1, 0, 2))
+    flip = core[None].astype(jnp.int32)
+
+    def by_head(part):
+        cut = project(normed, by_part, part, flip, cosine, sine, part < 2)
+        return exchange(cut.reshape(blocks, half, HD))
+
+    keys, values, query = by_head(1), by_head(2), by_head(0)
     swap = [(i, i ^ 1) for i in range(blocks)]
     k_other = lax.ppermute(keys, "blk", swap)
     v_other = lax.ppermute(values, "blk", swap)
-    all_pages = lax.all_gather(page_table, "blk", axis=0, tiled=False)
-    slots = all_pages.shape[1]
     core_pages = jnp.where(core == 0, all_pages[:, 0::2], all_pages[:, 1::2]).reshape(-1)
     starts = jnp.cumsum(prompt_lengths) - prompt_lengths
     info = jnp.concatenate([core[None], starts]).astype(jnp.int32)
-    heads_out, cache = attend(info, core_pages, query, keys, k_other, values, v_other)
-    heads_out = lax.all_to_all(heads_out, "blk", 0, 0, tiled=True).reshape(heads, 2, half, HD)
-    heads_out = jnp.where(block_id % 2 == 1, heads_out[:, ::-1], heads_out)
-    heads_out = jnp.transpose(heads_out, (1, 2, 0, 3)).reshape(rows, heads * HD)
-
-    attended = jnp.dot(heads_out, w_o, preferred_element_type=jnp.float32)
-    residual = tokens.astype(jnp.float32) + attended
-    moe_in = rms_scale(residual, moe_gain).astype(jnp.bfloat16)
+    cache = cache_pages(info, core_pages, keys, k_other, values, v_other)
+    cache, query = lax.optimization_barrier((cache, query))
+    cache = exchange(cache.reshape(blocks, slots // 2, 2, PAGE, HD))
+    heads_out = exchange(attend(info, query, keys, k_other, values, v_other))
+    residual, moe_in = attended_residual(
+        flip, heads_out.reshape(heads, 2, half, HD), w_o, tokens, moe_gain
+    )
 
     experts = experts_here * blocks
     cap = 5 * rows * TOP // (3 * experts)
     plane_experts = experts_here * PLANE
     plane_slots = plane_experts * cap
-    routing = lax.all_gather(
-        jnp.concatenate([expert_ids.astype(jnp.bfloat16), gate_weights], axis=1),
-        "blk",
-        axis=0,
-        tiled=False,
-        axis_index_groups=line_groups,
-    )
+    routings = jnp.stack(routings)
     named = (
-        routing[:, :, :TOP, None].astype(jnp.int32)
+        routings[:, :, :TOP, None].astype(jnp.int32)
         == plane_id * plane_experts + jnp.arange(plane_experts, dtype=jnp.int32)
     )
-    weight = jnp.sum(jnp.where(named, routing[:, :, TOP:, None].astype(jnp.float32), 0.0), axis=2)
+    weight = jnp.sum(jnp.where(named, routings[:, :, TOP:, None].astype(jnp.float32), 0.0), axis=2)
     named = jnp.any(named, axis=2)
     before = jnp.tril(jnp.ones((rows, rows), jnp.bfloat16), -1)
     rank = jnp.einsum(
@@ -442,61 +629,36 @@
         0.0,
     ).astype(jnp.bfloat16)
     chosen = chosen.astype(jnp.bfloat16)
-    gate_up = jnp.transpose(w_gate_up, (0, 2, 1, 3))
-
-    def to_plane(shift, rows_in):
-        source = (plane_id + shift) % planes
-        pick = lax.dynamic_index_in_dim(chosen, source, 0, keepdims=False)
+    tiles = ff // 128
+    gate_up = jnp.transpose(
+        w_gate_up.reshape(experts_here, width, 2, tiles, 128), (0, 3, 1, 2, 4)
+    ).reshape(experts_here, tiles, width, 256)
+
+    def plane_outputs(shift, rows_in):
         outgoing = lax.dot_general(
-            pick, rows_in, (((0,), (0,)), ((), ())), preferred_element_type=jnp.float32
+            chosen[shift], rows_in, (((0,), (0,)), ((), ())), preferred_element_type=jnp.float32
         ).astype(jnp.bfloat16)
-        return lax.all_to_all(
-            outgoing.reshape(PLANE, experts_here, cap, width),
-            "blk",
-            0,
-            0,
-            tiled=True,
-            axis_index_groups=plane_groups,
+        arrived = exchange(outgoing.reshape(PLANE, experts_here, cap, width), plane_groups)
+        inputs = jnp.transpose(arrived, (1, 0, 2, 3)).reshape(experts_here, PLANE * cap, width)
+        out = run_experts(inputs, gate_up, w_down).reshape(experts_here, PLANE, cap, width)
+        returned = exchange(jnp.transpose(out, (1, 0, 2, 3)), plane_groups)
+        return jnp.dot(
+            mixing[shift], returned.reshape(plane_slots, width), preferred_element_type=jnp.float32
         )
 
-    def run_experts(arrived):
-        inputs = jnp.transpose(arrived, (1, 0, 2, 3)).reshape(experts_here, PLANE * cap, width)
-        gate = jnp.einsum("end,edf->enf", inputs, gate_up[:, 0], preferred_element_type=jnp.float32)
-        up = jnp.einsum("end,edf->enf", inputs, gate_up[:, 1], preferred_element_type=jnp.float32)
-        hidden = (jax.nn.silu(gate) * up).astype(jnp.bfloat16)
-        out = jnp.einsum(
-            "enf,efd->end", hidden, w_down, preferred_element_type=jnp.float32
-        ).astype(jnp.bfloat16)
-        return jnp.transpose(out.reshape(experts_here, PLANE, cap, width), (1, 0, 2, 3))
-
-    def from_plane(shift, out):
-        source = (plane_id + shift) % planes
-        returned = lax.all_to_all(
-            out, "blk", 0, 0, tiled=True, axis_index_groups=plane_groups
-        ).reshape(plane_slots, width)
-        mix = lax.dynamic_index_in_dim(mixing, source, 0, keepdims=False)
-        return jnp.dot(mix, returned, preferred_element_type=jnp.float32)
-
-    def along_line(values, shift):
-        return lax.ppermute(
-            values, "blk", [(i, (i + shift * PLANE) % blocks) for i in range(blocks)]
-        )
-
-    order = [0, 1, 3, 2]
-    inputs = {s: moe_in if s == 0 else along_line(moe_in, -s) for s in order}
-    outs = {s: run_experts(to_plane(s, inputs[s])) for s in order}
-    mixed = residual
-    for s in [1, 3, 2, 0]:
-        part = from_plane(s, outs[s])
-        if s != 0:
-            part = along_line(part.astype(jnp.bfloat16), s).astype(jnp.float32)
-        mixed = mixed + part
-
-    cache = lax.all_to_all(
-        cache.reshape(blocks, slots // 2, 2, PAGE, HD), "blk", 0, 0, tiled=True
-    ).reshape(heads, 2, slots // 2, 2, PAGE, HD)
+    passing, parts = moe_in, {}
+    parts[0] = plane_outputs(0, passing)
+    for shift in range(planes - 1, 0, -1):
+        passing = along_line(passing, 1)
+        parts[shift] = plane_outputs(shift, passing)
+    total = parts[planes - 1]
+    for shift in range(planes - 2, -1, -1):
+        total = parts[shift] + along_line(total.astype(jnp.bfloat16), 1).astype(jnp.float32)
+    mixed = (residual + total).astype(jnp.bfloat16)
+
+    cache = cache.reshape(heads, 2, slots // 2, 2, PAGE, HD)
     kv_cache = jnp.transpose(cache, (2, 1, 3, 4, 0, 5)).reshape(slots, 2, PAGE, heads * HD)
-    return (mixed.astype(jnp.bfloat16), kv_cache)
+    return (mixed, kv_cache)
 
 
 def body(*args):

time: 749 us -> 743 us (level)
  Pallas kernels: 46.4 us -> 215 us
  matrix products: 167 us -> 25.3 us
  blocking collectives: 128 us -> 30.4 us
  local copies, waits for them, and re-layouts: 123 us -> 191 us
  waiting for transfers between devices: 197 us -> 183 us
  starting transfers between devices: 71.2 us -> 78.8 us
    pallas_call x1 -> x10, Pallas kernels: 46.4 us -> 215 us  [the longest x4 93.5 us: run_experts(): pl.pallas_call(experts_kernel, out_shape=jax.ShapeDtypeStruct((experts, r...]
    dot_general x24 -> x8, matrix products: 164 us -> 23 us  [the longest x4 12.6 us: plane_outputs(): jnp.dot(mixing[shift], returned.reshape(plane_slots, width), preferred_el...]
    transpose x4 -> x5, local copies, waits for them, and re-layouts: 12.5 us -> 68.6 us  [the longest x1 56 us: routed_body(): jnp.transpose(w_gate_up.reshape(experts_here, width, 2, tiles, 128), (0,...]
    dot_general x4 -> x0, local copies, waits for them, and re-layouts: 54 us -> none  [project(): jnp.dot(normed, w_qkv[:, part], preferred_element_type=jnp.float32)]
    all_gather x1 -> x0, blocking collectives: 53 us -> none  [routed_body(): lax.all_gather(jnp.concatenate([expert_ids.astype(jnp.bfloat16), gate_wei...]
    unnamed x1 -> x0, blocking collectives: 44.7 us -> none
    reshape x6 -> x5, local copies, waits for them, and re-layouts: 8.57 us -> 50.9 us  [the longest x1 36.6 us: routed_body(): gate_up = jnp.transpose(w_gate_up.reshape(experts_here, width, 2, tiles,...]
    unnamed x89 -> x36, local copies, waits for them, and re-layouts: 28.6 us -> 65.8 us
  transfers between devices with their start and end apart: 20 -> 24, of which waited for: 11 -> 15; matrix products, arithmetic and copies ran while one was open for 28% -> 29% of each run, Pallas kernels for 0% -> 25%
where the time goes in v2:
time: 743 us; the launch traced here: 736 us
  Pallas kernels  215 us (29%)
  local copies, waits for them, and re-layouts  191 us (26%)
  waiting for transfers between devices  183 us (25%)
  starting transfers between devices  78.8 us (11%)
  blocking collectives  30.4 us (4%)
  matrix products  25.3 us (3%)
  other arithmetic  11.4 us (2%)
    ppermute x9, waiting for transfers between devices, along_line(): lax.ppermute(values, 'blk', [(i, (i + shift * PLANE) % blocks) for i in r...  118 us
    pallas_call x4, Pallas kernels, run_experts(): pl.pallas_call(experts_kernel, out_shape=jax.ShapeDtypeStruct((experts, r...  93.5 us
    all_to_all x13, starting transfers between devices, exchange(): lax.all_to_all(values, 'blk', 0, 0, tiled=True, axis_index_groups=groups)  67.2 us
    pallas_call x1, Pallas kernels, cache_pages(): pl.pallas_call(cache_kernel, out_shape=jax.ShapeDtypeStruct((count, 2) +...  65.9 us
    unnamed x36, local copies, waits for them, and re-layouts  65.8 us
    all_to_all x13, waiting for transfers between devices, exchange(): lax.all_to_all(values, 'blk', 0, 0, tiled=True, axis_index_groups=groups)  62.9 us
    transpose x1, local copies, waits for them, and re-layouts, routed_body(): jnp.transpose(w_gate_up.reshape(experts_here, width, 2, tiles, 128), (0,...  56 us
    reshape x1, local copies, waits for them, and re-layouts, routed_body(): gate_up = jnp.transpose(w_gate_up.reshape(experts_here, width, 2, tiles,...  36.6 us
  transfers between devices with their start and end apart: 24, of which 15 were waited for; matrix products, arithmetic and copies ran while one was open for 29% of the time, Pallas kernels for 25%

profile of v2, /device:TPU:10, one launch (start us, length us, event | category | flops | bytes accessed | tf_op | source)
XLA Modules:
  0.0 736.4 jit_solution(5362204127549698759)
XLA Ops:
  1.9 6.0 all-to-all-start
  13.4 6.7 shard_map.122
  20.1 5.8 all-to-all-start.1
  25.9 6.3 shard_map.123
  32.3 18.4 %all-to-all-done.1.k_own = bf16[32,128,128]{2,1,0:T(8,128)(2,1)S(1)} async-done(((bf16[32,128,128]{2,1,0:T(8,128)(2,1)}), bf16[32,128,128]{2,1,0:T(8,128)(2,1)S(1)}, u32[]{:S(2)}, u32[]{:S(2)}) %all-to-all-start.1) | async-done | bytes 1048608 | tf_op jit(solution)/shard_map/all_to_all | solution.py:557
  50.7 5.1 all-to-all-start.2
  55.8 6.7 shard_map.125
  62.5 18.0 %all-to-all-done.2.v_own = bf16[32,128,128]{2,1,0:T(8,128)(2,1)S(1)} async-done(((bf16[32,128,128]{2,1,0:T(8,128)(2,1)}), bf16[32,128,128]{2,1,0:T(8,128)(2,1)S(1)}, u32[]{:S(2)}, u32[]{:S(2)}) %all-to-all-start.2) | async-done | bytes 1048608 | tf_op jit(solution)/shard_map/all_to_all | solution.py:557
  80.6 5.2 all-to-all-start.3
  90.1 65.9 %shard_map.124 = bf16[32,2,128,128]{3,2,1,0:T(8,128)(2,1)} custom-call(s32[5]{0:T(128)} %pad_add_fusion.info, s32[32]{0:T(128)} %fusion.35.pages, bf16[32,128,128]{2,1,0:T(8,128)(2,1)} %copy-done.2, bf16[32,128,128]{2,1,0:T(8,128)(2,1)} %collective-permute-done.k_other, bf16[32,128,128]{2,1,0:T(8,128)(2,1)} %copy-done.4, ...), custom_call_target="tpu_custom_call" | custom-call | bytes 4194304 | tf_op jit(solution)/shard_map/pallas_call | solution.py:296
  157.2 32.0 %shard_map.126 = bf16[32,128,128]{2,1,0:T(8,128)(2,1)S(1)} custom-call(s32[5]{0:T(128)S(1)} %copy-done.9, bf16[32,128,128]{2,1,0:T(8,128)(2,1)} %all-to-all-done.3.q_ref, bf16[32,128,128]{2,1,0:T(8,128)(2,1)S(1)} %copy-done.3, bf16[32,128,128]{2,1,0:T(8,128)(2,1)} %collective-permute-done.k_other, bf16[32,128,128]{2,1,0:T(8,128)(2,1)S(1)} %copy-done.5, ...), custom_call_target="tpu_custom_call" | custom-call | flops 20000000000 | bytes 10000000 | tf_op jit(solution)/shard_map/pallas_call | solution.py:395
  189.2 30.4 %all_to_all.70 = bf16[32,128,128]{2,1,0:T(8,128)(2,1)S(1)} all-to-all(bf16[32,128,128]{2,1,0:T(8,128)(2,1)S(1)} %shard_map.126), channel_id=1, replica_groups=mesh['blk'=32,'mp'=1] {'blk'}, dimensions={0} | all-to-all | bytes 2097152 | tf_op jit(solution)/shard_map/all_to_all | solution.py:557
  219.6 5.2 all-to-all-start.13
  229.4 41.7 %collective-permute-done.4 = bf16[256,12]{0,1:T(8,128)(2,1)S(1)} collective-permute-done((bf16[256,12]{0,1:T(8,128)(2,1)S(1)}, bf16[256,12]{0,1:T(8,128)(2,1)S(1)}, u32[]{:S(2)}, u32[]{:S(2)}) %collective-permute-start.4) | collective-permute-done | bytes 6176 | tf_op jit(solution)/shard_map/ppermute | solution.py:560
  275.0 3.4 copy-done.1
  278.4 4.2 shard_map.127
  283.9 3.2 convolution_convert_fusion.3
  287.1 5.0 all-to-all-start.5
  292.9 24.5 %collective-permute-done.5 = bf16[256,2048]{1,0:T(8,128)(2,1)S(1)} collective-permute-done((bf16[256,2048]{1,0:T(8,128)(2,1)S(1)}, bf16[256,2048]{1,0:T(8,128)(2,1)S(1)}, u32[]{:S(2)}, u32[]{:S(2)}) %collective-permute-start.5) | collective-permute-done | bytes 1048608 | tf_op jit(solution)/shard_map/ppermute | solution.py:560
  323.0 5.1 all-to-all-start.11
  328.8 24.7 %collective-permute-done.6 = bf16[256,2048]{1,0:T(8,128)(2,1)S(1)} collective-permute-done((bf16[256,2048]{1,0:T(8,128)(2,1)}, bf16[256,2048]{1,0:T(8,128)(2,1)S(1)}, u32[]{:S(2)}, u32[]{:S(2)}) %collective-permute-start.6) | collective-permute-done | bytes 1048608 | tf_op jit(solution)/shard_map/ppermute | solution.py:560
  360.4 5.8 all-to-all-start.9
  366.9 24.7 %collective-permute-done.7 = bf16[256,2048]{1,0:T(8,128)(2,1)S(1)} collective-permute-done((bf16[256,2048]{1,0:T(8,128)(2,1)}, bf16[256,2048]{1,0:T(8,128)(2,1)S(1)}, u32[]{:S(2)}, u32[]{:S(2)}) %collective-permute-start.7) | collective-permute-done | bytes 1048608 | tf_op jit(solution)/shard_map/ppermute | solution.py:560
  394.0 3.0 all-to-all-done.9
  397.0 5.1 all-to-all-start.7
  402.1 56.2 %copy.64 = bf16[2,2048,2,1408]{1,3,2,0:T(8,128)(2,1)} copy(bf16[2,2048,2,1408]{3,2,1,0:T(2,128)(2,1)} %param.16) | data formatting | bytes 46137344 | tf_op args[5]
  458.3 56.0 %copy.65 = bf16[2,11,2048,2,128]{4,3,2,1,0:T(2,128)(2,1)} copy(bf16[2,11,2048,2,128]{2,4,1,3,0:T(8,128)(2,1)} %bitcast.122) | data formatting | bytes 46137344 | tf_op jit(solution)/shard_map/transpose | solution.py:633
  514.2 36.6 %reshape.221.gate_up_hbm = bf16[2,11,2048,256]{3,2,1,0:T(8,128)(2,1)} reshape(bf16[2,11,2048,2,128]{4,3,2,1,0:T(2,128)(2,1)} %copy.65) | data formatting | bytes 46137344 | tf_op jit(solution)/shard_map/reshape | solution.py:635
  550.8 3.6 copy.71
  554.4 23.4 %shard_map.131 = bf16[2,320,2048]{2,1,0:T(8,128)(2,1)} custom-call(bf16[2,320,2048]{2,1,0:T(8,128)(2,1)} %bitcast.135, bf16[2,11,2048,256]{3,2,1,0:T(8,128)(2,1)} %reshape.221.gate_up_hbm, bf16[2,1408,2048]{2,1,0:T(8,128)(2,1)} %down_hbm.7), custom_call_target="tpu_custom_call" | custom-call | flops 11072962560 | bytes 39845888 | tf_op jit(solution)/shard_map/pallas_call | solution.py:509
  577.8 3.5 copy.80
  581.4 4.4 all-to-all-start.12
  585.8 3.6 copy.69
  589.4 23.4 %shard_map.130 = bf16[2,320,2048]{2,1,0:T(8,128)(2,1)} custom-call(bf16[2,320,2048]{2,1,0:T(8,128)(2,1)} %bitcast.137, bf16[2,11,2048,256]{3,2,1,0:T(8,128)(2,1)} %reshape.221.gate_up_hbm, bf16[2,1408,2048]{2,1,0:T(8,128)(2,1)} %down_hbm.7), custom_call_target="tpu_custom_call" | custom-call | flops 11072962560 | bytes 39845888 | tf_op jit(solution)/shard_map/pallas_call | solution.py:509
  612.7 3.6 copy.81
  616.7 5.8 all-to-all-start.10
  625.0 3.7 convolution_convert_fusion.4
  629.5 23.4 %shard_map.129 = bf16[2,320,2048]{2,1,0:T(8,128)(2,1)} custom-call(bf16[2,320,2048]{2,1,0:T(8,128)(2,1)} %bitcast.133, bf16[2,11,2048,256]{3,2,1,0:T(8,128)(2,1)} %reshape.221.gate_up_hbm, bf16[2,1408,2048]{2,1,0:T(8,128)(2,1)} %down_hbm.7), custom_call_target="tpu_custom_call" | custom-call | flops 11072962560 | bytes 39845888 | tf_op jit(solution)/shard_map/pallas_call | solution.py:509
  652.9 3.6 copy.82
  656.5 4.2 all-to-all-start.8
  660.7 3.6 copy.63
  664.3 4.1 add_convert_fusion.2
  670.0 23.4 %shard_map.128 = bf16[2,320,2048]{2,1,0:T(8,128)(2,1)} custom-call(bf16[2,320,2048]{2,1,0:T(8,128)(2,1)} %bitcast.132, bf16[2,11,2048,256]{3,2,1,0:T(8,128)(2,1)} %reshape.221.gate_up_hbm, bf16[2,1408,2048]{2,1,0:T(8,128)(2,1)} %down_hbm.7), custom_call_target="tpu_custom_call" | custom-call | flops 11072962560 | bytes 39845888 | tf_op jit(solution)/shard_map/pallas_call | solution.py:509
  693.3 3.5 copy.83
  696.9 4.6 all-to-all-start.6
  708.0 2.9 copy.74
  713.2 18.9 %all-to-all-done.6 = bf16[8,2,40,2048]{3,2,1,0:T(8,128)(2,1)} async-done(((bf16[8,2,40,2048]{3,2,1,0:T(8,128)(2,1)}), bf16[8,2,40,2048]{3,2,1,0:T(8,128)(2,1)}, u32[]{:S(2)}, u32[]{:S(2)}) %all-to-all-start.6) | async-done | bytes 2621472 | tf_op jit(solution)/shard_map/all_to_all | solution.py:557
  732.1 2.8 fusion.8
  (98 shorter events, 54.7 us)
Async XLA Ops:
  1.9 18.1 %all-to-all-start = ((bf16[32,8,128]{2,1,0:T(8,128)(2,1)}), bf16[32,8,128]{2,1,0:T(8,128)(2,1)S(1)}, u32[]{:S(2)}, u32[]{:S(2)}) async-start(bf16[32,8,128]{2,1,0:T(8,128)(2,1)} %broadcast_in_dim.65), calls=%async_computation | async-start | bytes 131072 | tf_op jit(solution)/shard_map/all_to_all | solution.py:557
  20.1 30.6 %all-to-all-start.1 = ((bf16[32,128,128]{2,1,0:T(8,128)(2,1)}), bf16[32,128,128]{2,1,0:T(8,128)(2,1)S(1)}, u32[]{:S(2)}, u32[]{:S(2)}) async-start(bf16[32,128,128]{2,1,0:T(8,128)(2,1)} %bitcast.8), calls=%async_computation.1 | async-start | bytes 2097152 | tf_op jit(solution)/shard_map/all_to_all | solution.py:557
  50.7 35.0 %copy-start.2 = (bf16[32,128,128]{2,1,0:T(8,128)(2,1)}, bf16[32,128,128]{2,1,0:T(8,128)(2,1)S(1)}, u32[]{:S(2)}) copy-start(bf16[32,128,128]{2,1,0:T(8,128)(2,1)S(1)} %all-to-all-done.1.k_own) | copy-start | bytes 3145732
  50.7 29.9 %all-to-all-start.2 = ((bf16[32,128,128]{2,1,0:T(8,128)(2,1)}), bf16[32,128,128]{2,1,0:T(8,128)(2,1)S(1)}, u32[]{:S(2)}, u32[]{:S(2)}) async-start(bf16[32,128,128]{2,1,0:T(8,128)(2,1)} %bitcast.9), calls=%async_computation.2 | async-start | bytes 2097152 | tf_op jit(solution)/shard_map/all_to_all | solution.py:557
  80.6 9.5 %copy-start.4 = (bf16[32,128,128]{2,1,0:T(8,128)(2,1)}, bf16[32,128,128]{2,1,0:T(8,128)(2,1)S(1)}, u32[]{:S(2)}) copy-start(bf16[32,128,128]{2,1,0:T(8,128)(2,1)S(1)} %all-to-all-done.2.v_own) | copy-start | bytes 3145732
  80.6 75.4 %all-to-all-start.3 = ((bf16[32,128,128]{2,1,0:T(8,128)(2,1)}), bf16[32,128,128]{2,1,0:T(8,128)(2,1)}, u32[]{:S(2)}, u32[]{:S(2)}) async-start(bf16[32,128,128]{2,1,0:T(8,128)(2,1)} %bitcast.10), calls=%async_computation.3 | async-start | bytes 2097152 | tf_op jit(solution)/shard_map/all_to_all | solution.py:557
  85.7 2.9 collective-permute-start
  85.9 4.1 collective-permute-start.1
  87.6 68.4 %copy-start.3 = (bf16[32,128,128]{2,1,0:T(8,128)(2,1)S(1)}, bf16[32,128,128]{2,1,0:T(8,128)(2,1)}, u32[]{:S(2)}) copy-start(bf16[32,128,128]{2,1,0:T(8,128)(2,1)} %copy-done.2) | copy-start | bytes 3145732
  87.6 68.4 %copy-start.9 = (s32[5]{0:T(128)S(1)}, s32[5]{0:T(128)}, u32[]{:S(2)}) copy-start(s32[5]{0:T(128)} %pad_add_fusion.info) | copy-start | bytes 64
  156.0 1.2 copy-start.5
  219.6 5.2 copy-start.15
  219.6 5.2 copy-start.16
  219.6 67.5 %all-to-all-start.13 = ((bf16[32,1,2,128,128]{4,3,2,1,0:T(8,128)(2,1)}), bf16[32,1,2,128,128]{4,3,2,1,0:T(8,128)(2,1)}, u32[]{:S(2)}, u32[]{:S(2)}) async-start(bf16[32,1,2,128,128]{4,3,2,1,0:T(8,128)(2,1)} %bitcast.131), calls=%async_computation.13 | async-start | bytes 4194304 | tf_op jit(solution)/shard_map/all_to_all | solution.py:557
  224.8 46.2 %collective-permute-start.4 = (bf16[256,12]{0,1:T(8,128)(2,1)S(1)}, bf16[256,12]{0,1:T(8,128)(2,1)S(1)}, u32[]{:S(2)}, u32[]{:S(2)}) collective-permute-start(bf16[256,12]{0,1:T(8,128)(2,1)S(1)} %get-tuple-element.13), channel_id=1, source_target_pairs={{0,8},{1,9},{2,10},{3,11},{4,12},{5,13},{6,14},{7,15},{8,16},{9,17... | collective-permute-start | bytes 18440 | tf_op jit(solution)/shard_map/ppermute | solution.py:560
  226.4 44.8 %collective-permute-start.3 = (bf16[256,12]{0,1:T(8,128)(2,1)S(1)}, bf16[256,12]{0,1:T(8,128)(2,1)S(1)}, u32[]{:S(2)}, u32[]{:S(2)}) collective-permute-start(bf16[256,12]{0,1:T(8,128)(2,1)S(1)} %get-tuple-element.13), channel_id=1, source_target_pairs={{0,16},{1,17},{2,18},{3,19},{4,20},{5,21},{6,22},{7,23},{8,24},{9,... | collective-permute-start | bytes 18440 | tf_op jit(solution)/shard_map/ppermute | solution.py:560
  227.8 45.3 %collective-permute-start.2 = (bf16[256,12]{0,1:T(8,128)(2,1)S(1)}, bf16[256,12]{0,1:T(8,128)(2,1)S(1)}, u32[]{:S(2)}, u32[]{:S(2)}) collective-permute-start(bf16[256,12]{0,1:T(8,128)(2,1)S(1)} %get-tuple-element.13), channel_id=1, source_target_pairs={{0,24},{1,25},{2,26},{3,27},{4,28},{5,29},{6,30},{7,31},{8,0},{9,1... | collective-permute-start | bytes 18440 | tf_op jit(solution)/shard_map/ppermute | solution.py:560
  273.2 1.8 copy-start
  273.2 1.7 copy-start.8
  275.0 3.4 copy-start.1
  282.5 1.4 copy-start.6
  287.1 31.2 %copy-start.12 = (pred[4,256,640]{2,1,0:T(32,128)(4,1)S(1)}, pred[4,256,640]{2,1,0:T(32,128)(4,1)}, u32[]{:S(2)}) copy-start(pred[4,256,640]{2,1,0:T(32,128)(4,1)} %convolution_compare_fusion) | copy-start | bytes 1966084
  287.1 35.9 %all-to-all-start.5 = ((bf16[8,2,40,2048]{3,2,1,0:T(8,128)(2,1)}), bf16[8,2,40,2048]{3,2,1,0:T(8,128)(2,1)}, u32[]{:S(2)}, u32[]{:S(2)}) async-start(bf16[8,2,40,2048]{3,2,1,0:T(8,128)(2,1)} %bitcast.123), calls=%async_computation.5 | async-start | bytes 5242880 | tf_op jit(solution)/shard_map/all_to_all | solution.py:557
  292.2 25.2 %collective-permute-start.5 = (bf16[256,2048]{1,0:T(8,128)(2,1)S(1)}, bf16[256,2048]{1,0:T(8,128)(2,1)S(1)}, u32[]{:S(2)}, u32[]{:S(2)}) collective-permute-start(bf16[256,2048]{1,0:T(8,128)(2,1)S(1)} %get-tuple-element.8), channel_id=1, source_target_pairs={{0,8},{1,9},{2,10},{3,11},{4,12},{5,13},{6,14},{7,15},{8,16},{9,17... | collective-permute-start | bytes 3145736 | tf_op jit(solution)/shard_map/ppermute | solution.py:560
  317.4 1.0 copy-start.13
  323.0 35.8 %all-to-all-start.11 = ((bf16[8,2,40,2048]{3,2,1,0:T(8,128)(2,1)}), bf16[8,2,40,2048]{3,2,1,0:T(8,128)(2,1)S(1)}, u32[]{:S(2)}, u32[]{:S(2)}) async-start(bf16[8,2,40,2048]{3,2,1,0:T(8,128)(2,1)} %bitcast.48), calls=%async_computation.11 | async-start | bytes 5242880 | tf_op jit(solution)/shard_map/all_to_all | solution.py:557
  328.1 25.4 %collective-permute-start.6 = (bf16[256,2048]{1,0:T(8,128)(2,1)}, bf16[256,2048]{1,0:T(8,128)(2,1)S(1)}, u32[]{:S(2)}, u32[]{:S(2)}) collective-permute-start(bf16[256,2048]{1,0:T(8,128)(2,1)} %copy-done.13), channel_id=1, source_target_pairs={{0,8},{1,9},{2,10},{3,11},{4,12},{5,13},{6,14},{7,15},{8,16},{9,17... | collective-permute-start | bytes 3145736 | tf_op jit(solution)/shard_map/ppermute | solution.py:560
  353.5 1.0 copy-start.14
  358.9 1.5 copy-start.10
  360.4 36.7 %all-to-all-start.9 = ((bf16[8,2,40,2048]{3,2,1,0:T(8,128)(2,1)}), bf16[8,2,40,2048]{3,2,1,0:T(8,128)(2,1)}, u32[]{:S(2)}, u32[]{:S(2)}) async-start(bf16[8,2,40,2048]{3,2,1,0:T(8,128)(2,1)} %bitcast.40), calls=%async_computation.9 | async-start | bytes 5242880 | tf_op jit(solution)/shard_map/all_to_all | solution.py:557
  366.2 25.4 %collective-permute-start.7 = (bf16[256,2048]{1,0:T(8,128)(2,1)}, bf16[256,2048]{1,0:T(8,128)(2,1)S(1)}, u32[]{:S(2)}, u32[]{:S(2)}) collective-permute-start(bf16[256,2048]{1,0:T(8,128)(2,1)} %copy-done.14), channel_id=1, source_target_pairs={{0,8},{1,9},{2,10},{3,11},{4,12},{5,13},{6,14},{7,15},{8,16},{9,17... | collective-permute-start | bytes 3145736 | tf_op jit(solution)/shard_map/ppermute | solution.py:560
  397.0 184.3 %all-to-all-start.7 = ((bf16[8,2,40,2048]{3,2,1,0:T(8,128)(2,1)}), bf16[8,2,40,2048]{3,2,1,0:T(8,128)(2,1)S(1)}, u32[]{:S(2)}, u32[]{:S(2)}) async-start(bf16[8,2,40,2048]{3,2,1,0:T(8,128)(2,1)} %bitcast.32), calls=%async_computation.7 | async-start | bytes 5242880 | tf_op jit(solution)/shard_map/all_to_all | solution.py:557
  581.4 35.3 %all-to-all-start.12 = ((bf16[8,2,40,2048]{3,2,1,0:T(8,128)(2,1)}), bf16[8,2,40,2048]{3,2,1,0:T(8,128)(2,1)}, u32[]{:S(2)}, u32[]{:S(2)}) async-start(bf16[8,2,40,2048]{3,2,1,0:T(8,128)(2,1)} %bitcast.130), calls=%async_computation.12 | async-start | bytes 5242880 | tf_op jit(solution)/shard_map/all_to_all | solution.py:557
  616.7 39.9 %all-to-all-start.10 = ((bf16[8,2,40,2048]{3,2,1,0:T(8,128)(2,1)}), bf16[8,2,40,2048]{3,2,1,0:T(8,128)(2,1)}, u32[]{:S(2)}, u32[]{:S(2)}) async-start(bf16[8,2,40,2048]{3,2,1,0:T(8,128)(2,1)} %bitcast.127), calls=%async_computation.10 | async-start | bytes 5242880 | tf_op jit(solution)/shard_map/all_to_all | solution.py:557
  623.1 1.9 copy-start.11
  628.8 35.6 %collective-permute-start.8 = (bf16[256,2048]{1,0:T(8,128)(2,1)}, bf16[256,2048]{1,0:T(8,128)(2,1)}, u32[]{:S(2)}, u32[]{:S(2)}) collective-permute-start(bf16[256,2048]{1,0:T(8,128)(2,1)} %convolution_convert_fusion.4), channel_id=1, source_target_pairs={{0,8},{1,9},{2,10},{3,11},{4,12},{5,13},{6,14},{7,15},{8,16},{9,17... | collective-permute-start | bytes 3145736 | tf_op jit(solution)/shard_map/ppermute | solution.py:560
  656.5 40.4 %all-to-all-start.8 = ((bf16[8,2,40,2048]{3,2,1,0:T(8,128)(2,1)}), bf16[8,2,40,2048]{3,2,1,0:T(8,128)(2,1)S(1)}, u32[]{:S(2)}, u32[]{:S(2)}) async-start(bf16[8,2,40,2048]{3,2,1,0:T(8,128)(2,1)} %bitcast.128), calls=%async_computation.8 | async-start | bytes 5242880 | tf_op jit(solution)/shard_map/all_to_all | solution.py:557
  668.4 35.0 %collective-permute-start.9 = (bf16[256,2048]{1,0:T(8,128)(2,1)}, bf16[256,2048]{1,0:T(8,128)(2,1)}, u32[]{:S(2)}, u32[]{:S(2)}) collective-permute-start(bf16[256,2048]{1,0:T(8,128)(2,1)} %add_convert_fusion.2), channel_id=1, source_target_pairs={{0,8},{1,9},{2,10},{3,11},{4,12},{5,13},{6,14},{7,15},{8,16},{9,17... | collective-permute-start | bytes 3145736 | tf_op jit(solution)/shard_map/ppermute | solution.py:560
  696.9 35.2 %all-to-all-start.6 = ((bf16[8,2,40,2048]{3,2,1,0:T(8,128)(2,1)}), bf16[8,2,40,2048]{3,2,1,0:T(8,128)(2,1)}, u32[]{:S(2)}, u32[]{:S(2)}) async-start(bf16[8,2,40,2048]{3,2,1,0:T(8,128)(2,1)} %bitcast.129), calls=%async_computation.6 | async-start | bytes 5242880 | tf_op jit(solution)/shard_map/all_to_all | solution.py:557
  706.0 28.9 %collective-permute-start.10 = (bf16[256,2048]{1,0:T(8,128)(2,1)}, bf16[256,2048]{1,0:T(8,128)(2,1)S(1)}, u32[]{:S(2)}, u32[]{:S(2)}) collective-permute-start(bf16[256,2048]{1,0:T(8,128)(2,1)} %add_convert_fusion.1), channel_id=1, source_target_pairs={{0,8},{1,9},{2,10},{3,11},{4,12},{5,13},{6,14},{7,15},{8,16},{9,17... | collective-permute-start | bytes 3145736 | tf_op jit(solution)/shard_map/ppermute | solution.py:560
  713.2 21.7 %copy-start.7 = (f32[256,2048]{1,0:T(8,128)S(1)}, f32[256,2048]{1,0:T(8,128)}, u32[]{:S(2)}) copy-start(f32[256,2048]{1,0:T(8,128)} %copy-done.6) | copy-start | bytes 6291460

commit v3 on v2

--- a/solution.py
+++ b/solution.py
@@ -220,6 +220,10 @@
 VMEM_BYTES = 56 * 2**20
 
 
+def after(values, *others):
+    return lax.optimization_barrier((values, others))[0]
+
+
 def project_kernel(turned, flip, x_ref, w_ref, cos_ref, sin_ref, out_ref):
     rows = x_ref.shape[0]
     half = rows // 2
@@ -256,49 +260,40 @@
     )(flip, normed, weights, cosine, sine)
 
 
-def cache_kernel(info, pages, k_own, k_other, v_own, v_other, out_ref, sems):
+def cache_kernel(info, pages, k_own, k_other, v_own, v_other, out_ref):
     sources = k_own.shape[0]
     core = info[0]
 
-    def copy(index, ref, which):
+    def one_page(index, _):
         page = pages[index]
         held = jnp.where(page < sources, page, 2 * sources - 1 - page)
-        return pltpu.make_async_copy(ref.at[held], out_ref.at[index, which], sems.at[index, which])
-
-    def start(index, _):
-        mine = (pages[index] + core) % 2 == 0
+        mine = (page + core) % 2 == 0
 
         @pl.when(mine)
         def _():
-            copy(index, k_own, 0).start()
-            copy(index, v_own, 1).start()
+            out_ref[index, 0] = k_own[held]
+            out_ref[index, 1] = v_own[held]
 
         @pl.when(jnp.logical_not(mine))
         def _():
-            copy(index, k_other, 0).start()
-            copy(index, v_other, 1).start()
+            out_ref[index, 0] = k_other[held]
+            out_ref[index, 1] = v_other[held]
 
         return 0
 
-    def finish(index, _):
-        copy(index, k_own, 0).wait()
-        copy(index, v_own, 1).wait()
-        return 0
-
-    lax.fori_loop(0, out_ref.shape[0], start, 0)
-    lax.fori_loop(0, out_ref.shape[0], finish, 0)
+    lax.fori_loop(0, out_ref.shape[0], one_page, 0)
 
 
 def cache_pages(info, pages, k_own, k_other, v_own, v_other):
     smem = pl.BlockSpec(memory_space=pltpu.SMEM)
-    anywhere = pl.BlockSpec(memory_space=pl.ANY)
+    vmem = pl.BlockSpec(memory_space=pltpu.VMEM)
     count = pages.shape[0]
     return pl.pallas_call(
         cache_kernel,
         out_shape=jax.ShapeDtypeStruct((count, 2) + k_own.shape[1:], jnp.bfloat16),
-        in_specs=[smem, smem] + [anywhere] * 4,
-        out_specs=anywhere,
-        scratch_shapes=[pltpu.SemaphoreType.DMA((count, 2))],
+        in_specs=[smem, smem] + [vmem] * 4,
+        out_specs=vmem,
+        compiler_params=pltpu.CompilerParams(vmem_limit_bytes=32 * 2**20),
         cost_estimate=pl.CostEstimate(flops=0, bytes_accessed=4 * k_own.size * 2, transcendentals=0),
     )(info, pages, k_own, k_other, v_own, v_other)
 
@@ -463,9 +458,12 @@
 def experts_kernel(x_ref, gate_up_hbm, down_hbm, out_ref, gate_up, down, hidden, gate_up_sems, down_sems):
     experts, tiles = gate_up.shape[:2]
 
-    def gate_up_copy(expert, tile):
+    def gate_up_copy(expert, tile, which):
+        at = pl.ds(pl.multiple_of(tile * 128, 128), 128)
         return pltpu.make_async_copy(
-            gate_up_hbm.at[expert, tile], gate_up.at[expert, tile], gate_up_sems.at[expert, tile]
+            gate_up_hbm.at[expert, which, :, at],
+            gate_up.at[expert, tile, :, pl.ds(which * 128, 128)],
+            gate_up_sems.at[expert, tile, which],
         )
 
     def down_copy(expert):
@@ -473,12 +471,14 @@
 
     for expert in range(experts):
         for tile in range(tiles):
-            gate_up_copy(expert, tile).start()
+            gate_up_copy(expert, tile, 0).start()
+            gate_up_copy(expert, tile, 1).start()
         down_copy(expert).start()
 
     def one_expert(expert, _):
         def one_tile(tile, _):
-            gate_up_copy(expert, tile).wait()
+            gate_up_copy(expert, tile, 0).wait()
+            gate_up_copy(expert, tile, 1).wait()
             both = jnp.dot(x_ref[expert], gate_up[expert, tile], preferred_element_type=jnp.float32)
             gate, up = both[:, :128], both[:, 128:]
             at = pl.ds(pl.multiple_of(tile * 128, 128), 128)
@@ -504,6 +504,7 @@
 def run_experts(inputs, gate_up, down):
     experts, rows, width = inputs.shape
     ff = down.shape[1]
+    tiles = ff // 128
     vmem = pl.BlockSpec(memory_space=pltpu.VMEM)
     anywhere = pl.BlockSpec(memory_space=pl.ANY)
     return pl.pallas_call(
@@ -512,10 +513,10 @@
         in_specs=[vmem, anywhere, anywhere],
         out_specs=vmem,
         scratch_shapes=[
-            pltpu.VMEM(gate_up.shape, jnp.bfloat16),
+            pltpu.VMEM((experts, tiles, width, 256), jnp.bfloat16),
             pltpu.VMEM(down.shape, jnp.bfloat16),
             pltpu.VMEM((rows, ff), jnp.bfloat16),
-            pltpu.SemaphoreType.DMA(gate_up.shape[:2]),
+            pltpu.SemaphoreType.DMA((experts, tiles, 2)),
             pltpu.SemaphoreType.DMA(down.shape[:1]),
         ],
         compiler_params=pltpu.CompilerParams(vmem_limit_bytes=VMEM_BYTES),
@@ -549,7 +550,6 @@
     planes = blocks // PLANE
     plane_id = block_id // PLANE
     experts_here = w_gate_up.shape[0]
-    ff = w_down.shape[1]
     slots = page_table.shape[0]
     plane_groups = [[z * PLANE + p for p in range(PLANE)] for z in range(planes)]
 
@@ -561,10 +561,14 @@
             values, "blk", [(i, (i + shift * PLANE) % blocks) for i in range(blocks)]
         )
 
-    page_rows = jnp.pad(page_table.astype(jnp.bfloat16)[None], ((0, 7), (0, 128 - slots)))
-    all_pages = exchange(jnp.broadcast_to(page_rows, (blocks, 8, 128)))[:, 0, :slots].astype(jnp.int32)
-    routing = jnp.concatenate([expert_ids.astype(jnp.bfloat16), gate_weights], axis=1)
-    routings = [routing] + [along_line(routing, -shift) for shift in range(1, planes)]
+    notes = jnp.concatenate(
+        [page_table.astype(jnp.bfloat16)]
+        + [part.astype(jnp.bfloat16).reshape(-1) for part in (expert_ids, gate_weights)]
+    )
+    named_count = rows * TOP
+    note_rows = -(-notes.shape[0] // 1024) * 8
+    notes = jnp.pad(notes, (0, note_rows * 128 - notes.shape[0])).reshape(note_rows, 128)
+    notes = exchange(jnp.broadcast_to(notes, (blocks, note_rows, 128))).reshape(blocks, -1)
 
     own_rows = block_id * rows + jnp.arange(rows, dtype=jnp.int32)
     own_pos = row_positions(own_rows, rows, blocks)
@@ -580,33 +584,20 @@
 
     def by_head(part):
         cut = project(normed, by_part, part, flip, cosine, sine, part < 2)
-        return exchange(cut.reshape(blocks, half, HD))
-
-    keys, values, query = by_head(1), by_head(2), by_head(0)
-    swap = [(i, i ^ 1) for i in range(blocks)]
-    k_other = lax.ppermute(keys, "blk", swap)
-    v_other = lax.ppermute(values, "blk", swap)
-    core_pages = jnp.where(core == 0, all_pages[:, 0::2], all_pages[:, 1::2]).reshape(-1)
-    starts = jnp.cumsum(prompt_lengths) - prompt_lengths
-    info = jnp.concatenate([core[None], starts]).astype(jnp.int32)
-    cache = cache_pages(info, core_pages, keys, k_other, values, v_other)
-    cache, query = lax.optimization_barrier((cache, query))
-    cache = exchange(cache.reshape(blocks, slots // 2, 2, PAGE, HD))
-    heads_out = exchange(attend(info, query, keys, k_other, values, v_other))
-    residual, moe_in = attended_residual(
-        flip, heads_out.reshape(heads, 2, half, HD), w_o, tokens, moe_gain
-    )
+        return cut.reshape(blocks, half, HD)
 
     experts = experts_here * blocks
     cap = 5 * rows * TOP // (3 * experts)
     plane_experts = experts_here * PLANE
     plane_slots = plane_experts * cap
-    routings = jnp.stack(routings)
+    line = (block_id + PLANE * jnp.arange(planes)) % blocks
+    routing = jnp.take(notes[:, slots : slots + 2 * named_count], line, axis=0)
+    ids = routing[:, :named_count].reshape(planes, rows, TOP).astype(jnp.int32)
+    gates = routing[:, named_count:].reshape(planes, rows, TOP).astype(jnp.float32)
     named = (
-        routings[:, :, :TOP, None].astype(jnp.int32)
-        == plane_id * plane_experts + jnp.arange(plane_experts, dtype=jnp.int32)
-    )
-    weight = jnp.sum(jnp.where(named, routings[:, :, TOP:, None].astype(jnp.float32), 0.0), axis=2)
+        ids[..., None] == plane_id * plane_experts + jnp.arange(plane_experts, dtype=jnp.int32)
+    )
+    weight = jnp.sum(jnp.where(named, gates[..., None], 0.0), axis=2)
     named = jnp.any(named, axis=2)
     before = jnp.tril(jnp.ones((rows, rows), jnp.bfloat16), -1)
     rank = jnp.einsum(
@@ -629,10 +620,27 @@
         0.0,
     ).astype(jnp.bfloat16)
     chosen = chosen.astype(jnp.bfloat16)
-    tiles = ff // 128
-    gate_up = jnp.transpose(
-        w_gate_up.reshape(experts_here, width, 2, tiles, 128), (0, 3, 1, 2, 4)
-    ).reshape(experts_here, tiles, width, 256)
+    values, keys = exchange(by_head(2)), exchange(by_head(1))
+    query = after(by_head(0), chosen, mixing)
+    w_gate_up, query = lax.optimization_barrier((w_gate_up, query))
+    gate_up, query = lax.optimization_barrier(
+        (jnp.transpose(w_gate_up, (0, 2, 1, 3)), exchange(query))
+    )
+    swap = [(i, i ^ 1) for i in range(blocks)]
+    k_other = lax.ppermute(keys, "blk", swap)
+    v_other = lax.ppermute(values, "blk", swap)
+    all_pages = notes[:, :slots].astype(jnp.int32)
+    core_pages = jnp.where(core == 0, all_pages[:, 0::2], all_pages[:, 1::2]).reshape(-1)
+    starts = jnp.cumsum(prompt_lengths) - prompt_lengths
+    info = jnp.concatenate([core[None], starts]).astype(jnp.int32)
+    cache = cache_pages(info, core_pages, keys, k_other, values, v_other)
+    cache, query = lax.optimization_barrier((cache, query))
+    cache = exchange(cache.reshape(blocks, slots // 2, 2, PAGE, HD))
+    heads_out = attend(info, query, keys, k_other, values, v_other)
+    heads_out = exchange(after(heads_out, cache))
+    residual, moe_in = attended_residual(
+        flip, heads_out.reshape(heads, 2, half, HD), w_o, tokens, moe_gain
+    )
 
     def plane_outputs(shift, rows_in):
         outgoing = lax.dot_general(

time: 743 us -> 522 us (0.70)
  local copies, waits for them, and re-layouts: 191 us -> 71 us
  Pallas kernels: 215 us -> 155 us
  waiting for transfers between devices: 183 us -> 146 us
    pallas_call x1, Pallas kernels: 65.9 us -> 4.04 us  [cache_pages(): pl.pallas_call(cache_kernel, out_shape=jax.ShapeDtypeStruct((count, 2) +...]
    unnamed x36 -> x28, local copies, waits for them, and re-layouts: 65.8 us -> 8.92 us
    transpose x1 -> x0, local copies, waits for them, and re-layouts: 56 us -> none  [routed_body(): jnp.transpose(w_gate_up.reshape(experts_here, width, 2, tiles, 128), (0,...]
    ppermute x9 -> x6, waiting for transfers between devices: 118 us -> 74.4 us  [along_line(): lax.ppermute(values, 'blk', [(i, (i + shift * PLANE) % blocks) for i in r...]
    reshape x1 -> x3, local copies, waits for them, and re-layouts: 36.6 us -> 0.31 us  [the longest x2 0.3 us: routed_body(): part.astype(jnp.bfloat16).reshape(-1)]
    optimization_barrier x0 -> x1, local copies, waits for them, and re-layouts: none -> 22 us  [routed_body(): w_gate_up, query = lax.optimization_barrier((w_gate_up, query))]
    all_to_all x13, waiting for transfers between devices: 62.9 us -> 71.2 us  [exchange(): lax.all_to_all(values, 'blk', 0, 0, tiled=True, axis_index_groups=groups)]
  transfers between devices with their start and end apart: 24 -> 21, of which waited for: 15 -> 11; matrix products, arithmetic and copies ran while one was open for 29% -> 18% of each run, Pallas kernels for 25% -> 28%
where the time goes in v3:
time: 522 us; the launch traced here: 517 us
  Pallas kernels  155 us (30%)
  waiting for transfers between devices  146 us (28%)
  starting transfers between devices  75.7 us (15%)
  local copies, waits for them, and re-layouts  71 us (14%)
  blocking collectives  31.1 us (6%)
  matrix products  26.4 us (5%)
  other arithmetic  10.9 us (2%)
    pallas_call x4, Pallas kernels, run_experts(): pl.pallas_call(experts_kernel, out_shape=jax.ShapeDtypeStruct((experts, r...  98.5 us
    ppermute x6, waiting for transfers between devices, along_line(): lax.ppermute(values, 'blk', [(i, (i + shift * PLANE) % blocks) for i in r...  74.4 us
    all_to_all x13, waiting for transfers between devices, exchange(): lax.all_to_all(values, 'blk', 0, 0, tiled=True, axis_index_groups=groups)  71.2 us
    all_to_all x13, starting transfers between devices, exchange(): lax.all_to_all(values, 'blk', 0, 0, tiled=True, axis_index_groups=groups)  68.9 us
    all_to_all x1, blocking collectives, exchange(): lax.all_to_all(values, 'blk', 0, 0, tiled=True, axis_index_groups=groups)  31.1 us
    pallas_call x1, Pallas kernels, attend(): pl.pallas_call(attend_kernel, out_shape=jax.ShapeDtypeStruct((sources, ha...  28.6 us
    optimization_barrier x1, local copies, waits for them, and re-layouts, routed_body(): w_gate_up, query = lax.optimization_barrier((w_gate_up, query))  22 us
    pallas_call x3, Pallas kernels, project(): pl.pallas_call(functools.partial(project_kernel, turned), grid=(heads //...  19.8 us
  transfers between devices with their start and end apart: 21, of which 11 were waited for; matrix products, arithmetic and copies ran while one was open for 18% of the time, Pallas kernels for 28%

profile of v3, /device:TPU:10, one launch (start us, length us, event | category | flops | bytes accessed | tf_op | source)
XLA Modules:
  0.0 516.9 jit_solution(178166532062550014)
XLA Ops:
  4.2 6.0 %all-to-all-start = ((bf16[32,32,128]{2,1,0:T(8,128)(2,1)}), bf16[32,32,128]{2,1,0:T(8,128)(2,1)S(1)}, u32[]{:S(2)}, u32[]{:S(2)}) async-start(bf16[32,32,128]{2,1,0:T(8,128)(2,1)} %broadcast_in_dim.71), calls=%async_computation | async-start | bytes 524288 | tf_op jit(solution)/shard_map/all_to_all | solution.py:557
  15.1 6.3 %shard_map.123 = bf16[16,2,128,128]{3,2,1,0:T(8,128)(2,1)} custom-call(s32[1]{0:T(128)} %bitcast.flip, bf16[256,2048]{1,0:T(8,128)(2,1)S(1)} %fusion.2.x_ref, bf16[3,2048,2048]{2,1,0:T(8,128)(2,1)} %bitcast.115, f32[256,128]{1,0:T(8,128)S(1)} %get-tuple-element.27.cos_ref, f32[256,128]{1,0:T(8,128)S(1)} %get-tuple-element.28.sin_ref), custom_call_target="tpu_custom_call" | custom-call | flops 2147483648 | bytes 8388608 | tf_op jit(solution)/shard_map/pallas_call | solution.py:244
  22.1 5.8 %all-to-all-start.2 = ((bf16[32,128,128]{2,1,0:T(8,128)(2,1)}), bf16[32,128,128]{2,1,0:T(8,128)(2,1)S(1)}, u32[]{:S(2)}, u32[]{:S(2)}) async-start(bf16[32,128,128]{2,1,0:T(8,128)(2,1)} %bitcast.6), calls=%async_computation.2 | async-start | bytes 2097152 | tf_op jit(solution)/shard_map/all_to_all | solution.py:557
  28.1 6.7 %shard_map.122 = bf16[16,2,128,128]{3,2,1,0:T(8,128)(2,1)} custom-call(s32[1]{0:T(128)} %bitcast.flip, bf16[256,2048]{1,0:T(8,128)(2,1)S(1)} %fusion.2.x_ref, bf16[3,2048,2048]{2,1,0:T(8,128)(2,1)} %bitcast.116, f32[256,128]{1,0:T(8,128)S(1)} %get-tuple-element.27.cos_ref, f32[256,128]{1,0:T(8,128)S(1)} %get-tuple-element.28.sin_ref), custom_call_target="tpu_custom_call" | custom-call | flops 2147483648 | bytes 8388608 | tf_op jit(solution)/shard_map/pallas_call | solution.py:244
  34.8 17.9 %all-to-all-done.2.v_own = bf16[32,128,128]{2,1,0:T(8,128)(2,1)S(1)} async-done(((bf16[32,128,128]{2,1,0:T(8,128)(2,1)}), bf16[32,128,128]{2,1,0:T(8,128)(2,1)S(1)}, u32[]{:S(2)}, u32[]{:S(2)}) %all-to-all-start.2) | async-done | bytes 1048608 | tf_op jit(solution)/shard_map/all_to_all | solution.py:557
  52.7 5.2 all-to-all-start.1
  57.9 6.8 %shard_map.125 = bf16[16,2,128,128]{3,2,1,0:T(8,128)(2,1)} custom-call(s32[1]{0:T(128)} %bitcast.flip, bf16[256,2048]{1,0:T(8,128)(2,1)S(1)} %fusion.2.x_ref, bf16[3,2048,2048]{2,1,0:T(8,128)(2,1)} %bitcast.117, f32[256,128]{1,0:T(8,128)S(1)} %get-tuple-element.27.cos_ref, f32[256,128]{1,0:T(8,128)S(1)} %get-tuple-element.28.sin_ref), custom_call_target="tpu_custom_call" | custom-call | flops 2147483648 | bytes 8388608 | tf_op jit(solution)/shard_map/pallas_call | solution.py:244
  69.6 13.1 %all-to-all-done.1.k_own = bf16[32,128,128]{2,1,0:T(8,128)(2,1)} async-done(((bf16[32,128,128]{2,1,0:T(8,128)(2,1)}), bf16[32,128,128]{2,1,0:T(8,128)(2,1)}, u32[]{:S(2)}, u32[]{:S(2)}) %all-to-all-start.1) | async-done | bytes 1048608 | tf_op jit(solution)/shard_map/all_to_all | solution.py:557
  82.7 5.1 all-to-all-start.3
  88.5 22.0 %copy.66 = bf16[2,2048,2,1408]{3,1,2,0:T(8,128)(2,1)} copy(bf16[2,2048,2,1408]{3,2,1,0:T(2,128)(2,1)} %param.16) | data formatting | bytes 46137344 | tf_op jit(solution)/shard_map/optimization_barrier | solution.py:625
  112.6 4.0 shard_map.124
  116.6 5.2 all-to-all-start.4
  121.8 28.6 %shard_map.126 = bf16[32,128,128]{2,1,0:T(8,128)(2,1)S(1)} custom-call(s32[5]{0:T(128)S(1)} %pad_add_fusion.info, bf16[32,128,128]{2,1,0:T(8,128)(2,1)S(1)} %all-to-all-done.3.q_ref, bf16[32,128,128]{2,1,0:T(8,128)(2,1)} %all-to-all-done.1.k_own, bf16[32,128,128]{2,1,0:T(8,128)(2,1)} %collective-permute-done.k_other, ...), custom_call_target="tpu_custom_call" | custom-call | flops 20000000000 | bytes 10000000 | tf_op jit(solution)/shard_map/pallas_call | solution.py:390
  151.3 17.0 %all-to-all-done.4 = bf16[32,1,2,128,128]{4,3,2,1,0:T(8,128)(2,1)} async-done(((bf16[32,1,2,128,128]{4,3,2,1,0:T(8,128)(2,1)}), bf16[32,1,2,128,128]{4,3,2,1,0:T(8,128)(2,1)}, u32[]{:S(2)}, u32[]{:S(2)}) %all-to-all-start.4) | async-done | bytes 2097184 | tf_op jit(solution)/shard_map/all_to_all | solution.py:557
  168.4 31.1 %all_to_all.70 = bf16[32,128,128]{2,1,0:T(8,128)(2,1)S(1)} all-to-all(bf16[32,128,128]{2,1,0:T(8,128)(2,1)} %copy-done.2), channel_id=1, replica_groups=mesh['blk'=32,'mp'=1] {'blk'}, dimensions={0} | all-to-all | bytes 2097152 | tf_op jit(solution)/shard_map/all_to_all | solution.py:557
  199.5 3.4 copy-done.1
  202.9 4.2 shard_map.127
  207.1 3.5 convolution_convert_fusion.3
  210.5 5.4 %all-to-all-start.6 = ((bf16[8,2,40,2048]{3,2,1,0:T(8,128)(2,1)}), bf16[8,2,40,2048]{3,2,1,0:T(8,128)(2,1)}, u32[]{:S(2)}, u32[]{:S(2)}) async-start(bf16[8,2,40,2048]{3,2,1,0:T(8,128)(2,1)} %bitcast.125), calls=%async_computation.6 | async-start | bytes 5242880 | tf_op jit(solution)/shard_map/all_to_all | solution.py:557
  216.6 24.7 %collective-permute-done.2 = bf16[256,2048]{1,0:T(8,128)(2,1)S(1)} collective-permute-done((bf16[256,2048]{1,0:T(8,128)(2,1)S(1)}, bf16[256,2048]{1,0:T(8,128)(2,1)S(1)}, u32[]{:S(2)}, u32[]{:S(2)}) %collective-permute-start.2) | collective-permute-done | bytes 1048608 | tf_op jit(solution)/shard_map/ppermute | solution.py:560
  242.2 3.2 convolution_convert_fusion
  246.9 6.0 %all-to-all-start.12 = ((bf16[8,2,40,2048]{3,2,1,0:T(8,128)(2,1)}), bf16[8,2,40,2048]{3,2,1,0:T(8,128)(2,1)}, u32[]{:S(2)}, u32[]{:S(2)}) async-start(bf16[8,2,40,2048]{3,2,1,0:T(8,128)(2,1)} %bitcast.123), calls=%async_computation.12 | async-start | bytes 5242880 | tf_op jit(solution)/shard_map/all_to_all | solution.py:557
  253.4 24.9 %collective-permute-done.3 = bf16[256,2048]{1,0:T(8,128)(2,1)S(1)} collective-permute-done((bf16[256,2048]{1,0:T(8,128)(2,1)}, bf16[256,2048]{1,0:T(8,128)(2,1)S(1)}, u32[]{:S(2)}, u32[]{:S(2)}) %collective-permute-start.3) | collective-permute-done | bytes 1048608 | tf_op jit(solution)/shard_map/ppermute | solution.py:560
  283.7 5.8 %all-to-all-start.10 = ((bf16[8,2,40,2048]{3,2,1,0:T(8,128)(2,1)}), bf16[8,2,40,2048]{3,2,1,0:T(8,128)(2,1)}, u32[]{:S(2)}, u32[]{:S(2)}) async-start(bf16[8,2,40,2048]{3,2,1,0:T(8,128)(2,1)} %bitcast.122), calls=%async_computation.10 | async-start | bytes 5242880 | tf_op jit(solution)/shard_map/all_to_all | solution.py:557
  290.0 24.9 %collective-permute-done.4 = bf16[256,2048]{1,0:T(8,128)(2,1)S(1)} collective-permute-done((bf16[256,2048]{1,0:T(8,128)(2,1)}, bf16[256,2048]{1,0:T(8,128)(2,1)S(1)}, u32[]{:S(2)}, u32[]{:S(2)}) %collective-permute-start.4) | collective-permute-done | bytes 1048608 | tf_op jit(solution)/shard_map/ppermute | solution.py:560
  317.3 3.1 all-to-all-done.10
  320.4 5.8 %all-to-all-start.8 = ((bf16[8,2,40,2048]{3,2,1,0:T(8,128)(2,1)}), bf16[8,2,40,2048]{3,2,1,0:T(8,128)(2,1)}, u32[]{:S(2)}, u32[]{:S(2)}) async-start(bf16[8,2,40,2048]{3,2,1,0:T(8,128)(2,1)} %bitcast.124), calls=%async_computation.8 | async-start | bytes 5242880 | tf_op jit(solution)/shard_map/all_to_all | solution.py:557
  326.2 3.5 copy.56
  329.7 24.6 %shard_map.131 = bf16[2,320,2048]{2,1,0:T(8,128)(2,1)} custom-call(bf16[2,320,2048]{2,1,0:T(8,128)(2,1)} %bitcast.133, bf16[2,2,2048,1408]{3,2,1,0:T(8,128)(2,1)} %bitcast.118, bf16[2,1408,2048]{2,1,0:T(8,128)(2,1)} %down_hbm.7), custom_call_target="tpu_custom_call" | custom-call | flops 11072962560 | bytes 39845888 | tf_op jit(solution)/shard_map/pallas_call | solution.py:510
  354.3 3.5 copy.67
  357.9 5.0 all-to-all-start.13
  362.8 3.5 copy.54
  366.4 24.6 %shard_map.130 = bf16[2,320,2048]{2,1,0:T(8,128)(2,1)} custom-call(bf16[2,320,2048]{2,1,0:T(8,128)(2,1)} %bitcast.135, bf16[2,2,2048,1408]{3,2,1,0:T(8,128)(2,1)} %bitcast.119, bf16[2,1408,2048]{2,1,0:T(8,128)(2,1)} %down_hbm.7), custom_call_target="tpu_custom_call" | custom-call | flops 11072962560 | bytes 39845888 | tf_op jit(solution)/shard_map/pallas_call | solution.py:510
  391.0 3.6 copy.68
  394.6 4.9 all-to-all-start.11
  399.5 3.5 copy.52
  403.1 3.8 convolution_convert_fusion.4
  407.4 24.6 %shard_map.129 = bf16[2,320,2048]{2,1,0:T(8,128)(2,1)} custom-call(bf16[2,320,2048]{2,1,0:T(8,128)(2,1)} %bitcast.131, bf16[2,2,2048,1408]{3,2,1,0:T(8,128)(2,1)} %bitcast.120, bf16[2,1408,2048]{2,1,0:T(8,128)(2,1)} %down_hbm.7), custom_call_target="tpu_custom_call" | custom-call | flops 11072962560 | bytes 39845888 | tf_op jit(solution)/shard_map/pallas_call | solution.py:510
  432.1 3.5 copy.69
  435.6 4.4 all-to-all-start.9
  440.0 3.5 copy.50
  444.5 3.1 add_convert_fusion.2
  449.0 24.7 %shard_map.128 = bf16[2,320,2048]{2,1,0:T(8,128)(2,1)} custom-call(bf16[2,320,2048]{2,1,0:T(8,128)(2,1)} %bitcast.130, bf16[2,2,2048,1408]{3,2,1,0:T(8,128)(2,1)} %bitcast.121, bf16[2,1408,2048]{2,1,0:T(8,128)(2,1)} %down_hbm.7), custom_call_target="tpu_custom_call" | custom-call | flops 11072962560 | bytes 39845888 | tf_op jit(solution)/shard_map/pallas_call | solution.py:510
  473.7 3.6 copy.70
  477.2 4.4 all-to-all-start.7
  489.6 4.3 copy.58
  493.8 4.2 reshape.313
  498.0 14.5 %all-to-all-done.7 = bf16[8,2,40,2048]{3,2,1,0:T(8,128)(2,1)} async-done(((bf16[8,2,40,2048]{3,2,1,0:T(8,128)(2,1)}), bf16[8,2,40,2048]{3,2,1,0:T(8,128)(2,1)}, u32[]{:S(2)}, u32[]{:S(2)}) %all-to-all-start.7) | async-done | bytes 2621472 | tf_op jit(solution)/shard_map/all_to_all | solution.py:557
  (94 shorter events, 44.9 us)
Async XLA Ops:
  0.6 12.8 %copy-start = (bf16[256,2048]{1,0:T(8,128)(2,1)S(1)}, bf16[256,2048]{1,0:T(8,128)(2,1)}, u32[]{:S(2)}) copy-start(bf16[256,2048]{1,0:T(8,128)(2,1)} %tokens_ref.1) | copy-start | bytes 3145732
  4.2 17.2 %all-to-all-start = ((bf16[32,32,128]{2,1,0:T(8,128)(2,1)}), bf16[32,32,128]{2,1,0:T(8,128)(2,1)S(1)}, u32[]{:S(2)}, u32[]{:S(2)}) async-start(bf16[32,32,128]{2,1,0:T(8,128)(2,1)} %broadcast_in_dim.71), calls=%async_computation | async-start | bytes 524288 | tf_op jit(solution)/shard_map/all_to_all | solution.py:557
  21.4 0.7 copy-start.9
  22.1 30.6 %all-to-all-start.2 = ((bf16[32,128,128]{2,1,0:T(8,128)(2,1)}), bf16[32,128,128]{2,1,0:T(8,128)(2,1)S(1)}, u32[]{:S(2)}, u32[]{:S(2)}) async-start(bf16[32,128,128]{2,1,0:T(8,128)(2,1)} %bitcast.6), calls=%async_computation.2 | async-start | bytes 2097152 | tf_op jit(solution)/shard_map/all_to_all | solution.py:557
  52.7 30.0 %all-to-all-start.1 = ((bf16[32,128,128]{2,1,0:T(8,128)(2,1)}), bf16[32,128,128]{2,1,0:T(8,128)(2,1)}, u32[]{:S(2)}, u32[]{:S(2)}) async-start(bf16[32,128,128]{2,1,0:T(8,128)(2,1)} %bitcast.5), calls=%async_computation.1 | async-start | bytes 2097152 | tf_op jit(solution)/shard_map/all_to_all | solution.py:557
  57.9 6.8 %copy-start.10 = (bf16[32,32,128]{2,1,0:T(8,128)(2,1)S(1)}, bf16[32,32,128]{2,1,0:T(8,128)(2,1)}, u32[]{:S(2)}) copy-start(bf16[32,32,128]{2,1,0:T(8,128)(2,1)} %copy-done.9) | copy-start | bytes 786436
  68.1 14.7 %copy-start.6 = (pred[4,256,640]{2,1,0:T(32,128)(4,1)}, pred[4,256,640]{2,1,0:T(32,128)(4,1)S(1)}, u32[]{:S(2)}) copy-start(pred[4,256,640]{2,1,0:T(32,128)(4,1)S(1)} %convolution_compare_fusion) | copy-start | bytes 1966084
  82.7 29.9 %all-to-all-start.3 = ((bf16[32,128,128]{2,1,0:T(8,128)(2,1)}), bf16[32,128,128]{2,1,0:T(8,128)(2,1)S(1)}, u32[]{:S(2)}, u32[]{:S(2)}) async-start(bf16[32,128,128]{2,1,0:T(8,128)(2,1)} %bitcast.7), calls=%async_computation.3 | async-start | bytes 2097152 | tf_op jit(solution)/shard_map/all_to_all | solution.py:557
  87.8 24.8 %collective-permute-start.1 = (bf16[32,128,128]{2,1,0:T(8,128)(2,1)S(1)}, bf16[32,128,128]{2,1,0:T(8,128)(2,1)}, u32[]{:S(2)}, u32[]{:S(2)}) collective-permute-start(bf16[32,128,128]{2,1,0:T(8,128)(2,1)S(1)} %all-to-all-done.2.v_own), channel_id=1, source_target_pairs={{0,1},{1,0},{2,3},{3,2},{4,5},{5,4},{6,7},{7,6},{8,9},{9,8},{10,11... | collective-permute-start | bytes 3145736 | tf_op jit(solution)/shard_map/ppermute | solution.py:631
  88.0 24.6 %collective-permute-start = (bf16[32,128,128]{2,1,0:T(8,128)(2,1)}, bf16[32,128,128]{2,1,0:T(8,128)(2,1)}, u32[]{:S(2)}, u32[]{:S(2)}) collective-permute-start(bf16[32,128,128]{2,1,0:T(8,128)(2,1)} %all-to-all-done.1.k_own), channel_id=1, source_target_pairs={{0,1},{1,0},{2,3},{3,2},{4,5},{5,4},{6,7},{7,6},{8,9},{9,8},{10,11... | collective-permute-start | bytes 3145736 | tf_op jit(solution)/shard_map/ppermute | solution.py:630
  116.6 51.7 %all-to-all-start.4 = ((bf16[32,1,2,128,128]{4,3,2,1,0:T(8,128)(2,1)}), bf16[32,1,2,128,128]{4,3,2,1,0:T(8,128)(2,1)}, u32[]{:S(2)}, u32[]{:S(2)}) async-start(bf16[32,1,2,128,128]{4,3,2,1,0:T(8,128)(2,1)} %bitcast.14), calls=%async_computation.4 | async-start | bytes 4194304 | tf_op jit(solution)/shard_map/all_to_all | solution.py:557
  121.8 77.7 %copy-start.5 = (f32[2048]{0:T(1024)S(1)}, f32[2048]{0:T(1024)}, u32[]{:S(2)}) copy-start(f32[2048]{0:T(1024)} %param.15) | copy-start | bytes 24580
  150.4 1.0 copy-start.2
  199.5 3.4 copy-start.1
  207.1 3.5 copy-start.3
  210.5 5.5 %copy-start.4 = (bf16[256,2048]{1,0:T(8,128)(2,1)S(1)}, bf16[256,2048]{1,0:T(8,128)(2,1)}, u32[]{:S(2)}) copy-start(bf16[256,2048]{1,0:T(8,128)(2,1)} %copy-done.3) | copy-start | bytes 3145732
  210.5 36.3 %all-to-all-start.6 = ((bf16[8,2,40,2048]{3,2,1,0:T(8,128)(2,1)}), bf16[8,2,40,2048]{3,2,1,0:T(8,128)(2,1)}, u32[]{:S(2)}, u32[]{:S(2)}) async-start(bf16[8,2,40,2048]{3,2,1,0:T(8,128)(2,1)} %bitcast.125), calls=%async_computation.6 | async-start | bytes 5242880 | tf_op jit(solution)/shard_map/all_to_all | solution.py:557
  216.0 25.2 %collective-permute-start.2 = (bf16[256,2048]{1,0:T(8,128)(2,1)S(1)}, bf16[256,2048]{1,0:T(8,128)(2,1)S(1)}, u32[]{:S(2)}, u32[]{:S(2)}) collective-permute-start(bf16[256,2048]{1,0:T(8,128)(2,1)S(1)} %copy-done.4), channel_id=1, source_target_pairs={{0,8},{1,9},{2,10},{3,11},{4,12},{5,13},{6,14},{7,15},{8,16},{9,17... | collective-permute-start | bytes 3145736 | tf_op jit(solution)/shard_map/ppermute | solution.py:560
  241.2 1.0 copy-start.11
  246.9 32.4 %copy-start.7 = (pred[4,256,640]{2,1,0:T(32,128)(4,1)S(1)}, pred[4,256,640]{2,1,0:T(32,128)(4,1)}, u32[]{:S(2)}) copy-start(pred[4,256,640]{2,1,0:T(32,128)(4,1)} %copy-done.6) | copy-start | bytes 1966084
  246.9 36.8 %all-to-all-start.12 = ((bf16[8,2,40,2048]{3,2,1,0:T(8,128)(2,1)}), bf16[8,2,40,2048]{3,2,1,0:T(8,128)(2,1)}, u32[]{:S(2)}, u32[]{:S(2)}) async-start(bf16[8,2,40,2048]{3,2,1,0:T(8,128)(2,1)} %bitcast.123), calls=%async_computation.12 | async-start | bytes 5242880 | tf_op jit(solution)/shard_map/all_to_all | solution.py:557
  252.8 25.4 %collective-permute-start.3 = (bf16[256,2048]{1,0:T(8,128)(2,1)}, bf16[256,2048]{1,0:T(8,128)(2,1)S(1)}, u32[]{:S(2)}, u32[]{:S(2)}) collective-permute-start(bf16[256,2048]{1,0:T(8,128)(2,1)} %copy-done.11), channel_id=1, source_target_pairs={{0,8},{1,9},{2,10},{3,11},{4,12},{5,13},{6,14},{7,15},{8,16},{9,17... | collective-permute-start | bytes 3145736 | tf_op jit(solution)/shard_map/ppermute | solution.py:560
  278.2 1.0 copy-start.12
  283.7 36.7 %all-to-all-start.10 = ((bf16[8,2,40,2048]{3,2,1,0:T(8,128)(2,1)}), bf16[8,2,40,2048]{3,2,1,0:T(8,128)(2,1)}, u32[]{:S(2)}, u32[]{:S(2)}) async-start(bf16[8,2,40,2048]{3,2,1,0:T(8,128)(2,1)} %bitcast.122), calls=%async_computation.10 | async-start | bytes 5242880 | tf_op jit(solution)/shard_map/all_to_all | solution.py:557
  289.5 25.4 %collective-permute-start.4 = (bf16[256,2048]{1,0:T(8,128)(2,1)}, bf16[256,2048]{1,0:T(8,128)(2,1)S(1)}, u32[]{:S(2)}, u32[]{:S(2)}) collective-permute-start(bf16[256,2048]{1,0:T(8,128)(2,1)} %copy-done.12), channel_id=1, source_target_pairs={{0,8},{1,9},{2,10},{3,11},{4,12},{5,13},{6,14},{7,15},{8,16},{9,17... | collective-permute-start | bytes 3145736 | tf_op jit(solution)/shard_map/ppermute | solution.py:560
  320.4 37.5 %all-to-all-start.8 = ((bf16[8,2,40,2048]{3,2,1,0:T(8,128)(2,1)}), bf16[8,2,40,2048]{3,2,1,0:T(8,128)(2,1)}, u32[]{:S(2)}, u32[]{:S(2)}) async-start(bf16[8,2,40,2048]{3,2,1,0:T(8,128)(2,1)} %bitcast.124), calls=%async_computation.8 | async-start | bytes 5242880 | tf_op jit(solution)/shard_map/all_to_all | solution.py:557
  357.9 36.7 %all-to-all-start.13 = ((bf16[8,2,40,2048]{3,2,1,0:T(8,128)(2,1)}), bf16[8,2,40,2048]{3,2,1,0:T(8,128)(2,1)}, u32[]{:S(2)}, u32[]{:S(2)}) async-start(bf16[8,2,40,2048]{3,2,1,0:T(8,128)(2,1)} %bitcast.129), calls=%async_computation.13 | async-start | bytes 5242880 | tf_op jit(solution)/shard_map/all_to_all | solution.py:557
  394.6 41.0 %all-to-all-start.11 = ((bf16[8,2,40,2048]{3,2,1,0:T(8,128)(2,1)}), bf16[8,2,40,2048]{3,2,1,0:T(8,128)(2,1)}, u32[]{:S(2)}, u32[]{:S(2)}) async-start(bf16[8,2,40,2048]{3,2,1,0:T(8,128)(2,1)} %bitcast.128), calls=%async_computation.11 | async-start | bytes 5242880 | tf_op jit(solution)/shard_map/all_to_all | solution.py:557
  406.9 36.7 %collective-permute-start.5 = (bf16[256,2048]{1,0:T(8,128)(2,1)}, bf16[256,2048]{1,0:T(8,128)(2,1)S(1)}, u32[]{:S(2)}, u32[]{:S(2)}) collective-permute-start(bf16[256,2048]{1,0:T(8,128)(2,1)} %convolution_convert_fusion.4), channel_id=1, source_target_pairs={{0,8},{1,9},{2,10},{3,11},{4,12},{5,13},{6,14},{7,15},{8,16},{9,17... | collective-permute-start | bytes 3145736 | tf_op jit(solution)/shard_map/ppermute | solution.py:560
  435.6 41.7 %all-to-all-start.9 = ((bf16[8,2,40,2048]{3,2,1,0:T(8,128)(2,1)}), bf16[8,2,40,2048]{3,2,1,0:T(8,128)(2,1)}, u32[]{:S(2)}, u32[]{:S(2)}) async-start(bf16[8,2,40,2048]{3,2,1,0:T(8,128)(2,1)} %bitcast.126), calls=%async_computation.9 | async-start | bytes 5242880 | tf_op jit(solution)/shard_map/all_to_all | solution.py:557
  443.6 1.0 copy-start.8
  447.6 36.9 %collective-permute-start.6 = (bf16[256,2048]{1,0:T(8,128)(2,1)S(1)}, bf16[256,2048]{1,0:T(8,128)(2,1)}, u32[]{:S(2)}, u32[]{:S(2)}) collective-permute-start(bf16[256,2048]{1,0:T(8,128)(2,1)S(1)} %add_convert_fusion.2), channel_id=1, source_target_pairs={{0,8},{1,9},{2,10},{3,11},{4,12},{5,13},{6,14},{7,15},{8,16},{9,17... | collective-permute-start | bytes 3145736 | tf_op jit(solution)/shard_map/ppermute | solution.py:560
  477.2 35.3 %all-to-all-start.7 = ((bf16[8,2,40,2048]{3,2,1,0:T(8,128)(2,1)}), bf16[8,2,40,2048]{3,2,1,0:T(8,128)(2,1)}, u32[]{:S(2)}, u32[]{:S(2)}) async-start(bf16[8,2,40,2048]{3,2,1,0:T(8,128)(2,1)} %bitcast.127), calls=%async_computation.7 | async-start | bytes 5242880 | tf_op jit(solution)/shard_map/all_to_all | solution.py:557
  487.0 28.3 %collective-permute-start.7 = (bf16[256,2048]{1,0:T(8,128)(2,1)}, bf16[256,2048]{1,0:T(8,128)(2,1)S(1)}, u32[]{:S(2)}, u32[]{:S(2)}) collective-permute-start(bf16[256,2048]{1,0:T(8,128)(2,1)} %add_convert_fusion.1), channel_id=1, source_target_pairs={{0,8},{1,9},{2,10},{3,11},{4,12},{5,13},{6,14},{7,15},{8,16},{9,17... | collective-permute-start | bytes 3145736 | tf_op jit(solution)/shard_map/ppermute | solution.py:560
